TPU v7x, 32 devices: a whole 2x2x4 slice. The times are simulated.
32 devices in a mesh: dp: 8 (over z, y), tensor: 4 (over x, core).
Axes of the slice: x: 2, y: 2, z: 4, core: 2. Of those that a mesh axis runs over, the one named last changes fastest.
Arguments:
- momentum: bfloat16 [8, 512, 8192], P(None, 'dp', 'tensor'), may hold values from -125 to 125
- master: float32 [8, 512, 8192], P(None, 'dp', 'tensor'), may hold values from -0.06 to 0.06
- owner_order: int32 [8], replicated, may hold values from 0 to 7, each once
Outputs:
- new_master: float32 [8, 512, 8192], P(None, 'dp', 'tensor')
- owned_update: bfloat16 [8, 512, 8192], P('dp', None, 'tensor')
Inputs may be any that keep to these rules, and one draw needn't show every extreme that they name: `owner_order`: each matrix appears in exactly one slot; slot j is owned by dp index j.
All inputs are finite; a program needn't handle non-finite values.
Results may differ from a plain program's by a relative error of at most 0.025.
Values may be sent and summed in bfloat16 or wider, within the bound.
A program may use at most 64 MiB of HBM per device.

v0:
```python
import math

import jax
import jax.numpy as jnp
from jax import lax
from jax.sharding import PartitionSpec as P

D = 8192
KV_DIM = 512
ITERS = 3


learn_rate = 0.02
weight_decay = 0.1
norm_epsilon = 1e-07
quintic_first = 3.4445
quintic_second = -4.775
quintic_third = 2.0315


def summed_gram(partial_value):
    return lax.psum(partial_value.astype(jnp.bfloat16), "tensor").astype(jnp.float32)


def shards(momentum, master, owner_order):
    matrices = momentum.shape[0]
    slotted = jnp.take(momentum, owner_order, axis=0)
    owned = lax.all_to_all(slotted, "dp", split_axis=0, concat_axis=1, tiled=True)
    squares = lax.psum(jnp.sum(jnp.square(owned.astype(jnp.float32)), axis=(1, 2)), "tensor")
    inv_norm = 1.0 / (jnp.sqrt(squares) + norm_epsilon)
    current = (owned.astype(jnp.float32) * inv_norm[:, None, None]).astype(jnp.bfloat16)
    source = owned
    combined = current.astype(jnp.float32)
    for iteration in range(ITERS):
        partial_value = jnp.einsum(
            "mik,mjk->mij", source, source, preferred_element_type=jnp.float32
        )
        gram = summed_gram(partial_value)
        if iteration == 0:
            gram = gram * (inv_norm * inv_norm)[:, None, None]
        coupling = gram.astype(jnp.bfloat16)
        first = jnp.einsum(
            "mij,mjk->mik", coupling, current, preferred_element_type=jnp.float32
        ).astype(jnp.bfloat16)
        second = jnp.einsum("mij,mjk->mik", coupling, first, preferred_element_type=jnp.float32)
        combined = (
            quintic_first * current.astype(jnp.float32)
            + quintic_second * first.astype(jnp.float32)
            + quintic_third * second
        )
        if iteration + 1 < ITERS:
            current = combined.astype(jnp.bfloat16)
            source = current
    scale_out = 0.2 * math.sqrt(max(KV_DIM, D))
    owned_update = (scale_out * combined).astype(jnp.bfloat16)
    returned = lax.all_to_all(owned_update, "dp", split_axis=1, concat_axis=0, tiled=True)
    inverse = (
        jnp.zeros((matrices,), jnp.int32).at[owner_order].set(jnp.arange(matrices, dtype=jnp.int32))
    )
    by_matrix = jnp.take(returned, inverse, axis=0)
    new_master = master * (1.0 - learn_rate * weight_decay) - learn_rate * by_matrix.astype(
        jnp.float32
    )
    return (new_master, owned_update)


def solution(mesh):
    return jax.shard_map(
        shards,
        mesh=mesh,
        in_specs=(P(None, "dp", "tensor"), P(None, "dp", "tensor"), P()),
        out_specs=(P(None, "dp", "tensor"), P("dp", None, "tensor")),
        check_vma=False,
    )
```

profile of v0, /device:TPU:0, one launch (start us, length us, event | category | flops | bytes accessed | tf_op | source)
XLA Modules:
  0.0 309.9 jit_solution(11322069004460484564)
XLA Ops:
  7.2 0.0 copy-start
  7.2 0.0 all-reduce.4.cloned.1.call-start
  7.2 0.8 compare_select_fusion.1
  8.0 0.7 compare_and_fusion.1
  8.7 0.1 copy-done
  8.8 2.0 gather_fusion
  10.8 1.9 broadcast_select_fusion
  12.6 55.3 %all_to_all.24 = bf16[8,64,2048]{2,1,0:T(8,128)(2,1)S(1)} all-to-all(bf16[8,64,2048]{2,1,0:T(8,128)(2,1)S(1)} %broadcast_select_fusion), channel_id=1, replica_groups=mesh['dp'=8,'tensor'=4] {'dp'}, dimensions={0} | all-to-all | bytes 4194304 | tf_op jit(solution)/shard_map/all_to_all | solution.py:28
  68.0 1.3 copy-done.1
  69.3 1.7 fusion
  70.9 6.3 %psum.28 = f32[1]{0:T(128)} all-reduce(f32[1]{0:T(128)} %bitcast.1), channel_id=1, replica_groups=mesh['dp'=8,'tensor'=4] {'tensor'}, use_global_device_ids=true, to_apply=%region_1.3 | all-reduce | flops 1 | bytes 8 | tf_op jit(solution)/shard_map/psum | solution.py:29
  77.9 4.3 %fusion.3 = bf16[1,512,512]{2,1,0:T(8,128)(2,1)} fusion(bf16[512,2048]{1,0:T(8,128)(2,1)} %bitcast.34), kind=kOutput, calls=%fused_computation.20 | convolution fusion | flops 1074003968 | bytes 2621440 | tf_op jit(solution)/shard_map/mik,mjk->mij/dot_general | solution.py:35
  82.2 0.0 all-reduce.4.cloned.1.call-update
  82.2 0.0 all-reduce.6.cloned.1.call-start
  82.3 3.4 %fusion.1 = bf16[8,64,2048]{2,1,0:T(8,128)(2,1)} fusion(bf16[8,64,2048]{2,1,0:T(8,128)(2,1)} %copy-done.1, f32[]{:T(128)} %bitcast.2), kind=kLoop, calls=%fused_computation.6 | loop fusion | flops 3145728 | bytes 4194308 | tf_op jit(solution)/shard_map/convert_element_type | solution.py:31
  85.8 29.0 %all-reduce.4.cloned.1.call-done = bf16[1,512,512]{2,1,0:T(8,128)(2,1)} async-done(((bf16[1,512,512]{2,1,0:T(8,128)(2,1)}), bf16[1,512,512]{2,1,0:T(8,128)(2,1)}) %all-reduce.4.cloned.1.call-update) | async-done | bytes 524304 | tf_op jit(solution)/shard_map/psum | solution.py:22
  114.8 3.2 %convolution_convert_fusion.2 = bf16[512,2048]{1,0:T(8,128)(2,1)S(1)} fusion(bf16[512,2048]{1,0:T(8,128)(2,1)} %bitcast.39, bf16[1,512,512]{2,1,0:T(8,128)(2,1)} %all-reduce.4.cloned.1.call-done, f32[]{:T(128)} %bitcast.4), kind=kOutput, calls=%fused_computation.14 | convolution fusion | flops 1075576832 | bytes 4718596 | tf_op jit(solution)/shard_map/mij,mjk->mik/dot_general | solution.py:42
  118.0 0.0 copy-done.2
  118.0 0.0 copy-done.4
  118.0 1.7 add_convert_fusion.1
  119.7 0.0 copy-start.7
  119.7 1.3 copy-done.7
  121.0 2.1 convolution_convert_fusion.4
  123.1 0.0 all-reduce.6.cloned.1.call-update
  123.1 0.2 all-reduce.8.cloned.1.call-start
  123.3 33.1 %all-reduce.6.cloned.1.call-done = bf16[512,512]{1,0:T(8,128)(2,1)} async-done(((bf16[512,512]{1,0:T(8,128)(2,1)}), bf16[512,512]{1,0:T(8,128)(2,1)}) %all-reduce.6.cloned.1.call-update) | async-done | bytes 524304 | tf_op jit(solution)/shard_map/psum | solution.py:22
  156.5 3.2 %convolution_convert_fusion.1 = bf16[512,2048]{1,0:T(8,128)(2,1)S(1)} fusion(bf16[512,512]{1,0:T(8,128)(2,1)} %all-reduce.6.cloned.1.call-done, bf16[512,2048]{1,0:T(8,128)(2,1)} %copy-done.7), kind=kOutput, calls=%fused_computation.13 | convolution fusion | flops 1074790400 | bytes 4718592 | tf_op jit(solution)/shard_map/mij,mjk->mik/dot_general | solution.py:42
  159.6 0.0 copy-done.5
  159.6 1.6 add_convert_fusion
  161.2 0.0 copy-start.9
  161.2 1.3 copy-done.9
  162.5 2.1 convolution_convert_fusion.3
  164.6 0.0 all-reduce.8.cloned.1.call-update
  164.6 33.4 %all-reduce.8.cloned.1.call-done = bf16[512,512]{1,0:T(8,128)(2,1)} async-done(((bf16[512,512]{1,0:T(8,128)(2,1)}), bf16[512,512]{1,0:T(8,128)(2,1)}) %all-reduce.8.cloned.1.call-update) | async-done | bytes 524304 | tf_op jit(solution)/shard_map/psum | solution.py:22
  198.0 3.2 %convolution_convert_fusion = bf16[512,2048]{1,0:T(8,128)(2,1)S(1)} fusion(bf16[512,512]{1,0:T(8,128)(2,1)} %all-reduce.8.cloned.1.call-done, bf16[512,2048]{1,0:T(8,128)(2,1)} %copy-done.9), kind=kOutput, calls=%fused_computation.12 | convolution fusion | flops 1074790400 | bytes 4718592 | tf_op jit(solution)/shard_map/mij,mjk->mik/dot_general | solution.py:42
  201.2 1.8 fusion.2
  202.9 0.0 copy-start.3
  202.9 5.2 %copy.9 = bf16[1,512,2048]{2,0,1:T(2,128)(2,1)} copy(bf16[1,512,2048]{2,1,0:T(8,128)(2,1)S(1)} %fusion.2) | data formatting | bytes 4194304 | tf_op jit(solution)/shard_map/convert_element_type | solution.py:55
  208.2 0.5 broadcast.93
  208.7 14.4 %reduce.1 = bf16[512,2048]{1,0:T(8,128)(2,1)} reduce(bf16[512,1,2048]{2,1,0:T(2,128)(2,1)} %bitcast.36, bf16[]{:T(256)} %broadcast.93), dimensions={1}, to_apply=%bitcast.33.reduce_sub_computation | reduce | bytes 4194306
  223.1 6.3 %reshape.144 = bf16[8,2,65536]{2,1,0:T(2,128)(2,1)} reshape(bf16[512,2048]{1,0:T(8,128)(2,1)} %reduce.1) | data formatting | bytes 4194304
  229.3 5.5 %all-to-all-start.1 = ((bf16[8,2,65536]{2,1,0:T(2,128)(2,1)}), bf16[8,2,65536]{2,1,0:T(2,128)(2,1)}, u32[]{:S(2)}, u32[]{:S(2)}) async-start(bf16[8,2,65536]{2,1,0:T(2,128)(2,1)} %reshape.144), calls=%async_computation.1 | async-start | bytes 4194304 | tf_op jit(solution)/shard_map/all_to_all | solution.py:56
  234.9 0.8 scatter_custom_fusion
  235.7 46.5 %all-to-all-done.1 = bf16[8,2,65536]{2,1,0:T(2,128)(2,1)} async-done(((bf16[8,2,65536]{2,1,0:T(2,128)(2,1)}), bf16[8,2,65536]{2,1,0:T(2,128)(2,1)}, u32[]{:S(2)}, u32[]{:S(2)}) %all-to-all-start.1) | async-done | bytes 2097184 | tf_op jit(solution)/shard_map/all_to_all | solution.py:56
  282.3 6.7 %reshape.145 = bf16[512,1,2048]{2,1,0:T(2,128)(2,1)} reshape(bf16[8,2,65536]{2,1,0:T(2,128)(2,1)} %all-to-all-done.1) | data formatting | bytes 4194304
  289.0 4.8 %copy.7 = bf16[1,512,2048]{2,1,0:T(8,128)(2,1)} copy(bf16[1,512,2048]{2,0,1:T(2,128)(2,1)} %bitcast.37) | data formatting | bytes 4194304
  293.8 3.6 %gather_fusion.1 = bf16[8,64,2048]{2,1,0:T(8,128)(2,1)} fusion(bf16[8,64,2048]{2,1,0:T(8,128)(2,1)} %bitcast.38, s32[1024]{0:T(1024)S(1)} %pad_clamp_fusion), kind=kCustom, calls=%fused_computation.1.clone | custom fusion | bytes 4194336 | tf_op jit(solution)/shard_map/jit(_take)/gather | solution.py:60
  297.4 6.0 %multiply_subtract_fusion = f32[8,64,2048]{2,1,0:T(8,128)} fusion(f32[8,64,2048]{2,1,0:T(8,128)} %param.6, bf16[8,64,2048]{2,1,0:T(8,128)(2,1)} %gather_fusion.1, pred[8]{0:T(512)(128)(4,1)S(1)} %compare_and_fusion), kind=kLoop, calls=%fused_computation.7 | loop fusion | flops 5242880 | bytes 10485768 | tf_op jit(solution)/shard_map/sub | solution.py:61
  (16 shorter events, 0.0 us)
Async XLA Ops:
  7.2 1.6 copy-start
  7.2 107.6 %all-reduce.4.cloned.1.call-start = ((), (), s32[]{:S(2)}) async-start(), calls=%async_computation.2 | async-start | bytes 1048576 | tf_op jit(solution)/shard_map/psum | solution.py:22
  68.0 1.3 copy-start.1
  82.2 74.2 %all-reduce.6.cloned.1.call-start = ((), (), s32[]{:S(2)}) async-start(), calls=%async_computation.3 | async-start | bytes 1048576 | tf_op jit(solution)/shard_map/psum | solution.py:22
  114.8 3.2 %copy-start.2 = (bf16[8,64,2048]{2,1,0:T(8,128)(2,1)S(1)}, bf16[8,64,2048]{2,1,0:T(8,128)(2,1)}, u32[]{:S(2)}) copy-start(bf16[8,64,2048]{2,1,0:T(8,128)(2,1)} %copy-done.1) | copy-start | bytes 6291460
  114.8 3.2 %copy-start.4 = (bf16[1,512,512]{2,1,0:T(8,128)(2,1)S(1)}, bf16[1,512,512]{2,1,0:T(8,128)(2,1)}, u32[]{:S(2)}) copy-start(bf16[1,512,512]{2,1,0:T(8,128)(2,1)} %all-reduce.4.cloned.1.call-done) | copy-start | bytes 1572868
  119.7 1.3 copy-start.7
  123.1 74.9 %all-reduce.8.cloned.1.call-start = ((), (), s32[]{:S(2)}) async-start(), calls=%async_computation.4 | async-start | bytes 1048576 | tf_op jit(solution)/shard_map/psum | solution.py:22
  156.5 3.2 %copy-start.5 = (bf16[512,512]{1,0:T(8,128)(2,1)S(1)}, bf16[512,512]{1,0:T(8,128)(2,1)}, u32[]{:S(2)}) copy-start(bf16[512,512]{1,0:T(8,128)(2,1)} %all-reduce.6.cloned.1.call-done) | copy-start | bytes 1572868
  156.5 3.2 %copy-start.8 = (bf16[512,2048]{1,0:T(8,128)(2,1)S(1)}, bf16[512,2048]{1,0:T(8,128)(2,1)}, u32[]{:S(2)}) copy-start(bf16[512,2048]{1,0:T(8,128)(2,1)} %copy-done.7) | copy-start | bytes 6291460
  161.2 1.3 copy-start.9
  198.0 3.2 %copy-start.6 = (bf16[512,512]{1,0:T(8,128)(2,1)S(1)}, bf16[512,512]{1,0:T(8,128)(2,1)}, u32[]{:S(2)}) copy-start(bf16[512,512]{1,0:T(8,128)(2,1)} %all-reduce.8.cloned.1.call-done) | copy-start | bytes 1572868
  198.0 3.2 %copy-start.10 = (bf16[512,2048]{1,0:T(8,128)(2,1)S(1)}, bf16[512,2048]{1,0:T(8,128)(2,1)}, u32[]{:S(2)}) copy-start(bf16[512,2048]{1,0:T(8,128)(2,1)} %copy-done.9) | copy-start | bytes 6291460
  202.9 5.3 %copy-start.3 = (bf16[1,512,2048]{2,1,0:T(8,128)(2,1)}, bf16[1,512,2048]{2,1,0:T(8,128)(2,1)S(1)}, u32[]{:S(2)}) copy-start(bf16[1,512,2048]{2,1,0:T(8,128)(2,1)S(1)} %fusion.2) | copy-start | bytes 6291460
  229.3 52.9 %all-to-all-start.1 = ((bf16[8,2,65536]{2,1,0:T(2,128)(2,1)}), bf16[8,2,65536]{2,1,0:T(2,128)(2,1)}, u32[]{:S(2)}, u32[]{:S(2)}) async-start(bf16[8,2,65536]{2,1,0:T(2,128)(2,1)} %reshape.144), calls=%async_computation.1 | async-start | bytes 4194304 | tf_op jit(solution)/shard_map/all_to_all | solution.py:56
Sparse Core Ops, SparseCore 0:
  82.4 32.3 all-reduce.3
  123.2 33.1 all-reduce.5
  164.8 33.1 all-reduce.7
where the time goes:
time: 311 us; the launch traced here: 310 us
  waiting for transfers between devices  142 us (46%)
  blocking collectives  61.6 us (20%)
  local copies, waits for them, and re-layouts  34 us (11%)
  other arithmetic  28.8 us (9%)
  matrix products  22.9 us (7%)
  between operations  14.7 us (5%)
  starting transfers between devices  5.82 us (2%)
    psum x3, waiting for transfers between devices, summed_gram(): lax.psum(partial_value.astype(jnp.bfloat16), 'tensor').astype(jnp.float32)  95.5 us
    all_to_all x1, blocking collectives, shards(): lax.all_to_all(slotted, 'dp', split_axis=0, concat_axis=1, tiled=True)  55.3 us
    all_to_all x1, waiting for transfers between devices, shards(): lax.all_to_all(owned_update, 'dp', split_axis=1, concat_axis=0, tiled=True)  46.5 us
    unnamed x26, local copies, waits for them, and re-layouts  22.4 us
    unnamed x1, other arithmetic  14.4 us
    dot_general x3, matrix products, shards(): jnp.einsum('mij,mjk->mik', coupling, current, preferred_element_type=jnp....  9.46 us
    dot_general x3, matrix products, shards(): jnp.einsum('mik,mjk->mij', source, source, preferred_element_type=jnp.flo...  8.45 us
    psum x1, blocking collectives, shards(): lax.psum(jnp.sum(jnp.square(owned.astype(jnp.float32)), axis=(1, 2)), 'te...  6.27 us
  transfers between devices with their start and end apart: 4, of which 4 were waited for; matrix products, arithmetic and copies ran while one was open for 1% of the time, Pallas kernels for 0%

commit v1 on v0

v1 whole, which is shorter than its diff:
```python
import math

import jax
import jax.numpy as jnp
from jax import lax
from jax.sharding import PartitionSpec as P

learn_rate = 0.02
weight_decay = 0.1
norm_epsilon = 1e-07
quintic_first = 3.4445
quintic_second = -4.775
quintic_third = 2.0315
ITERS = 3


def halves(value):
    high = value.astype(jnp.bfloat16)
    low = (value - high.astype(jnp.float32)).astype(jnp.bfloat16)
    return high, low


def narrow_dot(left, right):
    return jnp.dot(left, right, preferred_element_type=jnp.float32)


def split_dot(left, right):
    return (
        narrow_dot(left[0], right[0]) + narrow_dot(left[0], right[1]) + narrow_dot(left[1], right[0])
    )


def polynomial(gram):
    size = gram.shape[0]
    eye = jnp.eye(size, dtype=jnp.float32)
    whole = None
    for step in range(ITERS):
        gram_halves = halves(gram)
        square = split_dot(gram_halves, gram_halves)
        factor = quintic_first * eye + quintic_second * gram + quintic_third * square
        factor_halves = halves(factor)
        whole = factor if whole is None else split_dot(factor_halves, halves(whole))
        if step + 1 < ITERS:
            gram = split_dot(halves(split_dot(factor_halves, gram_halves)), factor_halves)
    return whole


def plain_shards(scale_out, momentum, master, owner_order):
    matrices = momentum.shape[0]
    slotted = jnp.take(momentum, owner_order, axis=0)
    owned = lax.all_to_all(slotted, "dp", split_axis=0, concat_axis=1, tiled=True)

    def one(matrix):
        squares = lax.psum(jnp.sum(jnp.square(matrix.astype(jnp.float32))), "tensor")
        inv_norm = 1.0 / (jnp.sqrt(squares) + norm_epsilon)
        partial_value = lax.dot_general(
            matrix, matrix, (((1,), (1,)), ((), ())), preferred_element_type=jnp.float32
        )
        gram = lax.psum(partial_value.astype(jnp.bfloat16), "tensor").astype(jnp.float32)
        whole = polynomial(gram * (inv_norm * inv_norm)) * (scale_out * inv_norm)
        high, low = halves(whole)
        return (narrow_dot(high, matrix) + narrow_dot(low, matrix)).astype(jnp.bfloat16)

    owned_update = jnp.stack([one(owned[index]) for index in range(owned.shape[0])])
    returned = lax.all_to_all(owned_update, "dp", split_axis=1, concat_axis=0, tiled=True)
    inverse = (
        jnp.zeros((matrices,), jnp.int32).at[owner_order].set(jnp.arange(matrices, dtype=jnp.int32))
    )
    by_matrix = jnp.take(returned, inverse, axis=0)
    new_master = master * (1.0 - learn_rate * weight_decay) - learn_rate * by_matrix.astype(
        jnp.float32
    )
    return (new_master, owned_update)


def solution(mesh):
    def whole_call(momentum, master, owner_order):
        scale_out = 0.2 * math.sqrt(max(momentum.shape[1], momentum.shape[2]))

        def shards(momentum, master, owner_order):
            return plain_shards(scale_out, momentum, master, owner_order)

        return jax.shard_map(
            shards,
            mesh=mesh,
            in_specs=(P(None, "dp", "tensor"), P(None, "dp", "tensor"), P()),
            out_specs=(P(None, "dp", "tensor"), P("dp", None, "tensor")),
            check_vma=False,
        )(momentum, master, owner_order)

    return whole_call
```

time: 311 us -> 218 us (0.70)
  waiting for transfers between devices: 142 us -> 70.3 us
  local copies, waits for them, and re-layouts: 34 us -> 22.4 us
  matrix products: 22.9 us -> 18.3 us
  other arithmetic: 28.8 us -> 24.3 us
    psum x3 -> x1, waiting for transfers between devices: 95.5 us -> 23.6 us  [one(): lax.psum(partial_value.astype(jnp.bfloat16), 'tensor').astype(jnp.float32)]
    unnamed x26 -> x12, local copies, waits for them, and re-layouts: 22.4 us -> 12.3 us
    another operation x0 -> x1, local copies, waits for them, and re-layouts: none -> 5.47 us  [plain_shards(): jnp.stack([one(owned[index]) for index in range(owned.shape[0])])]
    convert_element_type x1 -> x0, local copies, waits for them, and re-layouts: 5.25 us -> none  [shards(): owned_update = (scale_out * combined).astype(jnp.bfloat16)]
    dot_general x9 -> x30, matrix products: 22.9 us -> 18.3 us  [the longest x29 16.3 us: narrow_dot(): return jnp.dot(left, right, preferred_element_type=jnp.float32)]
    convert_element_type x1 -> x0, other arithmetic: 3.44 us -> none  [shards(): (owned.astype(jnp.float32) * inv_norm[:, None, None]).astype(jnp.bfloat16)]
  transfers between devices with their start and end apart: 4 -> 2, of which waited for: 4 -> 2; matrix products, arithmetic and copies ran while one was open for 1% -> 1% of each run, Pallas kernels for 0% -> 0%
where the time goes in v1:
time: 218 us; the launch traced here: 217 us
  waiting for transfers between devices  70.3 us (32%)
  blocking collectives  61.6 us (28%)
  other arithmetic  24.3 us (11%)
  local copies, waits for them, and re-layouts  22.4 us (10%)
  matrix products  18.3 us (8%)
  between operations  15 us (7%)
  starting transfers between devices  5.55 us (3%)
    all_to_all x1, blocking collectives, plain_shards(): lax.all_to_all(slotted, 'dp', split_axis=0, concat_axis=1, tiled=True)  55.3 us
    all_to_all x1, waiting for transfers between devices, plain_shards(): lax.all_to_all(owned_update, 'dp', split_axis=1, concat_axis=0, tiled=True)  46.7 us
    psum x1, waiting for transfers between devices, one(): lax.psum(partial_value.astype(jnp.bfloat16), 'tensor').astype(jnp.float32)  23.6 us
    dot_general x29, matrix products, narrow_dot(): return jnp.dot(left, right, preferred_element_type=jnp.float32)  16.3 us
    unnamed x1, other arithmetic  13.2 us
    unnamed x12, local copies, waits for them, and re-layouts  12.3 us
    psum x1, blocking collectives, one(): lax.psum(jnp.sum(jnp.square(matrix.astype(jnp.float32))), 'tensor')  6.27 us
    sub x1, other arithmetic, plain_shards(): master * (1.0 - learn_rate * weight_decay)  6.09 us
  transfers between devices with their start and end apart: 2, of which 2 were waited for; matrix products, arithmetic and copies ran while one was open for 1% of the time, Pallas kernels for 0%

profile of v1, /device:TPU:0, one launch (start us, length us, event | category | flops | bytes accessed | tf_op | source)
XLA Modules:
  0.0 217.5 jit_solution(16901918074642383720)
XLA Ops:
  7.2 0.8 compare_select_fusion.1
  8.0 0.7 compare_and_fusion.1
  8.8 2.0 gather_fusion
  10.8 1.9 broadcast_select_fusion
  12.6 55.3 %all_to_all.21 = bf16[8,64,2048]{2,1,0:T(8,128)(2,1)S(1)} all-to-all(bf16[8,64,2048]{2,1,0:T(8,128)(2,1)S(1)} %broadcast_select_fusion), channel_id=1, replica_groups=mesh['dp'=8,'tensor'=4] {'dp'}, dimensions={0} | all-to-all | bytes 4194304 | tf_op jit(solution)/shard_map/all_to_all | solution.py:51
  68.0 2.1 convolution_convert_fusion
  70.1 1.7 multiply_reduce_fusion
  71.7 6.3 %psum.15 = f32[]{:T(128)} all-reduce(f32[]{:T(128)} %multiply_reduce_fusion), channel_id=1, replica_groups=mesh['dp'=8,'tensor'=4] {'tensor'}, use_global_device_ids=true, to_apply=%region_2.4 | all-reduce | flops 1 | bytes 8 | tf_op jit(solution)/shard_map/psum | solution.py:54
  78.7 23.6 %all-reduce.2.cloned.1.call-done = bf16[512,512]{1,0:T(8,128)(2,1)} async-done(((bf16[512,512]{1,0:T(8,128)(2,1)}), bf16[512,512]{1,0:T(8,128)(2,1)}) %all-reduce.2.cloned.1.call-update) | async-done | bytes 524304 | tf_op jit(solution)/shard_map/psum | solution.py:59
  102.4 1.7 fusion.14
  104.1 0.5 convolution_add_fusion.17
  104.6 0.6 subtract_convert_fusion.8
  105.2 0.5 fusion.10
  105.6 0.5 convolution_add_fusion.15
  106.1 0.5 convolution_add_fusion.14
  106.6 0.4 fusion.44
  107.0 0.4 convolution_add_fusion.13
  107.5 0.5 convolution_add_fusion.12
  107.9 0.4 fusion.52
  108.4 0.4 convolution_add_fusion.11
  108.8 0.5 subtract_convert_fusion.5
  109.4 0.4 fusion.47
  110.3 0.4 convolution_add_fusion.9
  110.7 0.4 convolution_add_fusion.8
  111.2 0.4 fusion.40
  111.6 0.4 convolution_add_fusion.7
  112.1 0.5 convolution_add_fusion.6
  112.5 0.4 fusion.24
  113.0 0.4 convolution_add_fusion.5
  113.4 0.5 fusion.3
  113.9 0.4 convolution_add_fusion.3
  114.4 0.4 convolution_add_fusion.2
  114.8 0.5 fusion.33
  115.3 0.5 convolution_add_fusion.1
  115.8 0.4 fusion.1
  116.2 1.3 fusion.27
  117.5 1.3 fusion
  118.8 5.5 %copy.9 = bf16[1,512,2048]{2,0,1:T(2,128)(2,1)} copy(bf16[1,512,2048]{2,1,0:T(8,128)(2,1)S(1)} %fusion) | data formatting | bytes 4194304 | tf_op jit(solution)/shard_map/stack | solution.py:64
  124.3 0.6 broadcast.84
  124.9 13.2 %reduce.1 = bf16[512,2048]{1,0:T(8,128)(2,1)S(1)} reduce(bf16[512,1,2048]{2,1,0:T(2,128)(2,1)} %bitcast.33, bf16[]{:T(256)} %broadcast.84), dimensions={1}, to_apply=%bitcast.29.reduce_sub_computation | reduce | bytes 4194306
  138.1 3.8 %reshape.49 = bf16[8,2,65536]{2,1,0:T(2,128)(2,1)} reshape(bf16[512,2048]{1,0:T(8,128)(2,1)S(1)} %reduce.1) | data formatting | bytes 4194304
  141.9 5.5 %all-to-all-start.1 = ((bf16[8,2,65536]{2,1,0:T(2,128)(2,1)}), bf16[8,2,65536]{2,1,0:T(2,128)(2,1)S(1)}, u32[]{:S(2)}, u32[]{:S(2)}) async-start(bf16[8,2,65536]{2,1,0:T(2,128)(2,1)} %reshape.49), calls=%async_computation.1 | async-start | bytes 4194304 | tf_op jit(solution)/shard_map/all_to_all | solution.py:65
  147.4 0.6 scatter_custom_fusion
  148.0 46.7 %all-to-all-done.1 = bf16[8,2,65536]{2,1,0:T(2,128)(2,1)S(1)} async-done(((bf16[8,2,65536]{2,1,0:T(2,128)(2,1)}), bf16[8,2,65536]{2,1,0:T(2,128)(2,1)S(1)}, u32[]{:S(2)}, u32[]{:S(2)}) %all-to-all-start.1) | async-done | bytes 2097184 | tf_op jit(solution)/shard_map/all_to_all | solution.py:65
  194.7 4.3 %reshape.50 = bf16[512,1,2048]{2,1,0:T(2,128)(2,1)} reshape(bf16[8,2,65536]{2,1,0:T(2,128)(2,1)S(1)} %all-to-all-done.1) | data formatting | bytes 4194304
  199.0 3.5 %copy.7 = bf16[1,512,2048]{2,1,0:T(8,128)(2,1)S(1)} copy(bf16[1,512,2048]{2,0,1:T(2,128)(2,1)} %bitcast.34) | data formatting | bytes 4194304
  202.5 2.0 gather_fusion.1
  204.5 6.1 %multiply_subtract_fusion = f32[8,64,2048]{2,1,0:T(8,128)} fusion(f32[8,64,2048]{2,1,0:T(8,128)} %param.6, bf16[8,64,2048]{2,1,0:T(8,128)(2,1)} %gather_fusion.1, pred[8]{0:T(512)(128)(4,1)S(1)} %compare_and_fusion), kind=kLoop, calls=%fused_computation.3 | loop fusion | flops 5242880 | bytes 10485768 | tf_op jit(solution)/shard_map/sub | solution.py:70
  (16 shorter events, 0.6 us)
Async XLA Ops:
  7.2 1.6 copy-start
  7.2 95.2 %all-reduce.2.cloned.1.call-start = ((), (), s32[]{:S(2)}) async-start(), calls=%async_computation.2 | async-start | bytes 1048576 | tf_op jit(solution)/shard_map/psum | solution.py:59
  102.4 1.7 copy-start.2
  118.8 5.5 %copy-start.3 = (bf16[1,512,2048]{2,1,0:T(8,128)(2,1)}, bf16[1,512,2048]{2,1,0:T(8,128)(2,1)S(1)}, u32[]{:S(2)}) copy-start(bf16[1,512,2048]{2,1,0:T(8,128)(2,1)S(1)} %fusion) | copy-start | bytes 6291460
  141.9 52.8 %all-to-all-start.1 = ((bf16[8,2,65536]{2,1,0:T(2,128)(2,1)}), bf16[8,2,65536]{2,1,0:T(2,128)(2,1)S(1)}, u32[]{:S(2)}, u32[]{:S(2)}) async-start(bf16[8,2,65536]{2,1,0:T(2,128)(2,1)} %reshape.49), calls=%async_computation.1 | async-start | bytes 4194304 | tf_op jit(solution)/shard_map/all_to_all | solution.py:65
  204.5 6.1 %copy-start.1 = (bf16[8,64,2048]{2,1,0:T(8,128)(2,1)S(1)}, bf16[8,64,2048]{2,1,0:T(8,128)(2,1)}, u32[]{:S(2)}) copy-start(bf16[8,64,2048]{2,1,0:T(8,128)(2,1)} %param.5) | copy-start | bytes 6291460
Sparse Core Ops, SparseCore 0:
  70.2 32.1 all-reduce.1

commit v2 on v1

--- a/solution.py
+++ b/solution.py
@@ -1,8 +1,11 @@
+import functools
 import math
 
 import jax
 import jax.numpy as jnp
 from jax import lax
+from jax.experimental import pallas as pl
+from jax.experimental.pallas import tpu as pltpu
 from jax.sharding import PartitionSpec as P
 
 learn_rate = 0.02
@@ -12,6 +15,7 @@
 quintic_second = -4.775
 quintic_third = 2.0315
 ITERS = 3
+MESH = pl.DeviceIdType.MESH
 
 
 def halves(value):
@@ -24,24 +28,285 @@
     return jnp.dot(left, right, preferred_element_type=jnp.float32)
 
 
-def split_dot(left, right):
-    return (
-        narrow_dot(left[0], right[0]) + narrow_dot(left[0], right[1]) + narrow_dot(left[1], right[0])
-    )
+def transposed_dot(left, right):
+    return lax.dot_general(
+        left, right, (((1,), (1,)), ((), ())), preferred_element_type=jnp.float32
+    )
+
+
+def far_first(count):
+    return sorted(range(1, count), key=lambda offset: (abs(2 * offset - count), -offset))
+
+
+def owner_kernel(
+    n, rows, cols, chunk, scale_out,
+    order_ref, mom_ref, ret_ref, upd_ref,
+    send, recv, upd, gram, acc, part, part_in, half_out, half_in,
+    gram_hi, gram_lo, fac_hi, fac_lo, all_hi, all_lo, tmp_hi, tmp_lo,
+    in_send, in_recv, sum_send, sum_recv, out_send, out_recv, local_sem,
+):
+    me = lax.axis_index("dp")
+    lane = lax.axis_index("tensor")
+    core = lax.rem(lane, 2)
+    mate = lane + 1 - 2 * core
+    across = lax.rem(lane + 2, 4)
+    size = n * rows
+    half = size // 2
+    chunks = cols // chunk
+
+    barrier = pltpu.get_barrier_semaphore()
+    for offset in range(1, n):
+        pl.semaphore_signal(
+            barrier, inc=1, device_id=(lax.rem(me + offset, n), lane), device_id_type=MESH
+        )
+    for other in (mate, across):
+        pl.semaphore_signal(barrier, inc=1, device_id=(me, other), device_id_type=MESH)
+    pl.semaphore_wait(barrier, n + 1)
+
+    def rows_in(offset, index):
+        place = pl.ds(index * chunk, chunk)
+        return pltpu.make_async_remote_copy(
+            src_ref=send.at[offset - 1, :, place],
+            dst_ref=recv.at[me, :, place],
+            send_sem=in_send.at[offset - 1, index],
+            recv_sem=in_recv.at[offset - 1, index],
+            device_id=(lax.rem(me + offset, n), lane),
+            device_id_type=MESH,
+        )
+
+    for index in range(chunks):
+        for offset in far_first(n):
+            if index == 0:
+                send[offset - 1] = mom_ref[order_ref[lax.rem(me + offset, n)]]
+            rows_in(offset, index).start()
+    recv[me] = mom_ref[order_ref[me]]
+
+    acc[...] = jnp.zeros_like(acc)
+
+    def add_chunk(index, carry):
+        place = pl.ds(pl.multiple_of(index * chunk, chunk), chunk)
+        for offset in range(1, n):
+            pltpu.make_async_remote_copy(
+                src_ref=send.at[offset - 1, :, place],
+                dst_ref=recv.at[lax.rem(me + n - offset, n), :, place],
+                send_sem=in_send.at[offset - 1, index],
+                recv_sem=in_recv.at[offset - 1, index],
+                device_id=(lax.rem(me + offset, n), lane),
+                device_id_type=MESH,
+            ).wait_recv()
+        block = recv[:, :, place].reshape(size, chunk)
+        for start in (0, half):
+            acc[start : start + half, :] += transposed_dot(block[start : start + half], block)
+        return carry
+
+    lax.fori_loop(0, chunks, add_chunk, 0)
+
+    part[...] = acc[...].astype(jnp.bfloat16)
+    swap = pltpu.make_async_remote_copy(
+        src_ref=part, dst_ref=part_in, send_sem=sum_send.at[0], recv_sem=sum_recv.at[0],
+        device_id=(me, mate), device_id_type=MESH,
+    )
+    swap.start()
+    swap.wait()
+    mine = pl.ds(pl.multiple_of(core * half, half), half)
+    half_out[...] = (
+        part[mine, :].astype(jnp.float32) + part_in[mine, :].astype(jnp.float32)
+    ).astype(jnp.bfloat16)
+    swap = pltpu.make_async_remote_copy(
+        src_ref=half_out, dst_ref=half_in, send_sem=sum_send.at[1], recv_sem=sum_recv.at[1],
+        device_id=(me, across), device_id_type=MESH,
+    )
+    swap.start()
+    swap.wait()
+    gram[mine, :] = half_out[...].astype(jnp.float32) + half_in[...].astype(jnp.float32)
+    swap = pltpu.make_async_remote_copy(
+        src_ref=gram.at[mine, :], dst_ref=gram.at[mine, :],
+        send_sem=sum_send.at[2], recv_sem=sum_recv.at[2],
+        device_id=(me, mate), device_id_type=MESH,
+    )
+    swap.start()
+    swap.wait()
+
+    def diagonal(start):
+        row = start + lax.broadcasted_iota(jnp.int32, (half, size), 0)
+        return row == lax.broadcasted_iota(jnp.int32, (half, size), 1)
+
+    strips = [(start, slice(start, start + half)) for start in (0, half)]
+    squares = sum(
+        jnp.sum(jnp.where(diagonal(start), gram[strip, :], 0.0), keepdims=True)
+        for start, strip in strips
+    )
+    inv_norm = 1.0 / (jnp.sqrt(squares) + norm_epsilon)
+    for start, strip in strips:
+        scaled = gram[strip, :] * (inv_norm * inv_norm)
+        acc[strip, :] = scaled
+        gram_hi[strip, :], gram_lo[strip, :] = halves(scaled)
+
+    for step in range(ITERS):
+        last = step + 1 == ITERS
+        for start, strip in strips:
+            square = (
+                narrow_dot(gram_hi[strip, :], gram_hi[...])
+                + narrow_dot(gram_hi[strip, :], gram_lo[...])
+                + narrow_dot(gram_lo[strip, :], gram_hi[...])
+            )
+            factor = quintic_second * acc[strip, :] + quintic_third * square
+            factor += jnp.where(diagonal(start), quintic_first, 0.0)
+            fac_hi[strip, :], fac_lo[strip, :] = halves(factor)
+            if step == 0:
+                all_hi[strip, :], all_lo[strip, :] = halves(factor)
+        if not last:
+            for start, strip in strips:
+                tmp_hi[strip, :] = narrow_dot(fac_hi[strip, :], gram_hi[...]).astype(jnp.bfloat16)
+            for start, strip in strips:
+                following = narrow_dot(tmp_hi[strip, :], fac_hi[...])
+                acc[strip, :] = following
+                gram_hi[strip, :], gram_lo[strip, :] = halves(following)
+        if step > 0:
+            for start, strip in strips:
+                joined = (
+                    narrow_dot(fac_hi[strip, :], all_hi[...])
+                    + narrow_dot(fac_hi[strip, :], all_lo[...])
+                    + narrow_dot(fac_lo[strip, :], all_hi[...])
+                )
+                if last:
+                    joined = joined * (scale_out * inv_norm)
+                tmp_hi[strip, :], tmp_lo[strip, :] = halves(joined)
+            if not last:
+                all_hi[...] = tmp_hi[...]
+                all_lo[...] = tmp_lo[...]
+
+    def rows_out(dest):
+        return pltpu.make_async_remote_copy(
+            src_ref=upd.at[pl.ds(pl.multiple_of(dest * rows, rows), rows), :],
+            dst_ref=ret_ref.at[me],
+            send_sem=out_send.at[dest],
+            recv_sem=out_recv.at[me],
+            device_id=(dest, lane),
+            device_id_type=MESH,
+        )
+
+    pairs = n // 2
+    pair = lax.div(me, 2)
+    twin = me + 1 - 2 * lax.rem(me, 2)
+    for offset in far_first(pairs) + [0]:
+        first = 2 * lax.rem(pair + offset, pairs)
+        place = pl.ds(pl.multiple_of(first * rows, 2 * rows), 2 * rows)
+
+        def apply_chunk(index, carry):
+            lanes = pl.ds(pl.multiple_of(index * chunk, chunk), chunk)
+            block = recv[:, :, lanes].reshape(size, chunk)
+            upd[place, lanes] = (
+                narrow_dot(tmp_hi[place, :], block) + narrow_dot(tmp_lo[place, :], block)
+            ).astype(jnp.bfloat16)
+            return carry
+
+        lax.fori_loop(0, chunks, apply_chunk, 0)
+        if offset:
+            rows_out(first).start()
+            rows_out(first + 1).start()
+        else:
+            rows_out(twin).start()
+    own = pltpu.make_async_copy(
+        upd.at[pl.ds(pl.multiple_of(me * rows, rows), rows), :], ret_ref.at[me], local_sem.at[0]
+    )
+    own.start()
+    whole = pltpu.make_async_copy(upd, upd_ref, local_sem.at[1])
+    whole.start()
+
+    for index in range(chunks):
+        for offset in range(1, n):
+            rows_in(offset, index).wait_send()
+    own.wait()
+    whole.wait()
+    for offset in range(1, n):
+        dest = lax.rem(me + offset, n)
+        rows_out(dest).wait_send()
+        pltpu.make_async_remote_copy(
+            src_ref=upd.at[pl.ds(pl.multiple_of(dest * rows, rows), rows), :],
+            dst_ref=ret_ref.at[dest],
+            send_sem=out_send.at[dest],
+            recv_sem=out_recv.at[dest],
+            device_id=(dest, lane),
+            device_id_type=MESH,
+        ).wait_recv()
+
+
+def owner_call(scale_out, n, momentum, owner_order):
+    rows, cols = momentum.shape[1:]
+    size, half = n * rows, n * rows // 2
+    chunk = cols // 4
+    square_16 = pltpu.VMEM((size, size), jnp.bfloat16)
+    square_32 = pltpu.VMEM((size, size), jnp.float32)
+    half_16 = pltpu.VMEM((half, size), jnp.bfloat16)
+    dma = pltpu.SemaphoreType.DMA
+    return pl.pallas_call(
+        functools.partial(owner_kernel, n, rows, cols, chunk, scale_out),
+        out_shape=(
+            jax.ShapeDtypeStruct((n, rows, cols), jnp.bfloat16),
+            jax.ShapeDtypeStruct((size, cols), jnp.bfloat16),
+        ),
+        in_specs=[
+            pl.BlockSpec(memory_space=pltpu.SMEM),
+            pl.BlockSpec(memory_space=pltpu.VMEM),
+        ],
+        out_specs=(pl.BlockSpec(memory_space=pl.ANY), pl.BlockSpec(memory_space=pl.ANY)),
+        scratch_shapes=[
+            pltpu.VMEM((n - 1, rows, cols), jnp.bfloat16),
+            pltpu.VMEM((n, rows, cols), jnp.bfloat16),
+            pltpu.VMEM((size, cols), jnp.bfloat16),
+            square_32, square_32, square_16, square_16, half_16, half_16,
+            square_16, square_16, square_16, square_16, square_16, square_16, square_16, square_16,
+            dma((n - 1, 4)), dma((n - 1, 4)), dma((3,)), dma((3,)), dma((n,)), dma((n,)), dma((2,)),
+        ],
+        compiler_params=pltpu.CompilerParams(
+            collective_id=0, has_side_effects=True, vmem_limit_bytes=48 << 20
+        ),
+    )(owner_order, momentum)
+
+
+def master_kernel(order_ref, ret_ref, master_ref, out_ref):
+    out_ref[...] = master_ref[...] * (1.0 - learn_rate * weight_decay) - learn_rate * ret_ref[
+        ...
+    ].astype(jnp.float32)
+
+
+def master_call(returned, master, owner_order):
+    n, rows, cols = master.shape
+    by_slot = pl.BlockSpec((1, rows, cols), lambda slot, order: (slot, 0, 0))
+    by_matrix = pl.BlockSpec((1, rows, cols), lambda slot, order: (order[slot], 0, 0))
+    return pl.pallas_call(
+        master_kernel,
+        out_shape=jax.ShapeDtypeStruct(master.shape, jnp.float32),
+        grid_spec=pltpu.PrefetchScalarGridSpec(
+            num_scalar_prefetch=1,
+            grid=(n,),
+            in_specs=[by_slot, by_matrix],
+            out_specs=by_matrix,
+        ),
+        compiler_params=pltpu.CompilerParams(vmem_limit_bytes=32 << 20),
+    )(owner_order, returned, master)
+
+
+def kernel_shards(scale_out, n, momentum, master, owner_order):
+    returned, owned_update = owner_call(scale_out, n, momentum, owner_order)
+    return master_call(returned, master, owner_order), owned_update[None]
+
+
+def wide_dot(left, right):
+    return jnp.dot(left, right, precision=lax.Precision.HIGH)
 
 
 def polynomial(gram):
-    size = gram.shape[0]
-    eye = jnp.eye(size, dtype=jnp.float32)
+    eye = jnp.eye(gram.shape[0], dtype=jnp.float32)
     whole = None
     for step in range(ITERS):
-        gram_halves = halves(gram)
-        square = split_dot(gram_halves, gram_halves)
-        factor = quintic_first * eye + quintic_second * gram + quintic_third * square
-        factor_halves = halves(factor)
-        whole = factor if whole is None else split_dot(factor_halves, halves(whole))
+        factor = (
+            quintic_first * eye + quintic_second * gram + quintic_third * wide_dot(gram, gram)
+        )
+        whole = factor if whole is None else wide_dot(factor, whole)
         if step + 1 < ITERS:
-            gram = split_dot(halves(split_dot(factor_halves, gram_halves)), factor_halves)
+            gram = wide_dot(wide_dot(factor, gram), factor)
     return whole
 
 
@@ -58,8 +323,7 @@
         )
         gram = lax.psum(partial_value.astype(jnp.bfloat16), "tensor").astype(jnp.float32)
         whole = polynomial(gram * (inv_norm * inv_norm)) * (scale_out * inv_norm)
-        high, low = halves(whole)
-        return (narrow_dot(high, matrix) + narrow_dot(low, matrix)).astype(jnp.bfloat16)
+        return wide_dot(whole, matrix.astype(jnp.float32)).astype(jnp.bfloat16)
 
     owned_update = jnp.stack([one(owned[index]) for index in range(owned.shape[0])])
     returned = lax.all_to_all(owned_update, "dp", split_axis=1, concat_axis=0, tiled=True)
@@ -74,10 +338,15 @@
 
 
 def solution(mesh):
+    n, lanes = mesh.shape["dp"], mesh.shape["tensor"]
+
     def whole_call(momentum, master, owner_order):
         scale_out = 0.2 * math.sqrt(max(momentum.shape[1], momentum.shape[2]))
 
         def shards(momentum, master, owner_order):
+            matrices, rows, cols = momentum.shape
+            if matrices == n and lanes == 4 and rows % 16 == 0 and cols % 512 == 0:
+                return kernel_shards(scale_out, n, momentum, master, owner_order)
             return plain_shards(scale_out, momentum, master, owner_order)
 
         return jax.shard_map(

time: 218 us -> 127 us (0.58)
  the two profiles are of different devices: /device:TPU:0 before, /device:TPU:13 now
where the time goes in v2:
time: 127 us
  Pallas kernels  122 us (96%)
  local copies, waits for them, and re-layouts  4.15 us (3%)
    pallas_call x1, Pallas kernels, owner_call(): pl.pallas_call(functools.partial(owner_kernel, n, rows, cols, chunk, scal...  118 us
    pallas_call x1, Pallas kernels, master_call(): pl.pallas_call(master_kernel, out_shape=jax.ShapeDtypeStruct(master.shape...  4.21 us
    unnamed x5, local copies, waits for them, and re-layouts  4.15 us

profile of v2, /device:TPU:13, one launch (start us, length us, event | category | flops | bytes accessed | tf_op | source)
XLA Modules:
  0.0 126.8 jit_solution(16832623561701243988)
XLA Ops:
  0.6 0.0 copy-start.1
  0.6 0.6 copy-done.1
  1.3 117.8 %shard_map.50 = (bf16[8,64,2048]{2,1,0:T(8,128)(2,1)S(1)}, bf16[512,2048]{1,0:T(8,128)(2,1)S(1)}) custom-call(s32[8]{0:T(128)S(1)} %copy-done.1, bf16[8,64,2048]{2,1,0:T(8,128)(2,1)} %mom_ref.1), custom_call_target="tpu_custom_call" | custom-call | tf_op jit(solution)/shard_map/pallas_call | solution.py:243
  119.1 0.0 copy-start
  119.1 2.2 %copy-done = f32[8,64,2048]{2,1,0:T(8,128)S(1)} copy-done((f32[8,64,2048]{2,1,0:T(8,128)S(1)}, f32[8,64,2048]{2,1,0:T(8,128)}, u32[]{:S(2)}) %copy-start) | copy-done | bytes 4194328
  121.3 4.2 %shard_map.51 = f32[8,64,2048]{2,1,0:T(8,128)} custom-call(s32[8]{0:T(128)S(1)} %copy-done.1, bf16[8,64,2048]{2,1,0:T(8,128)(2,1)S(1)} %get-tuple-element.4.ret_ref, f32[8,64,2048]{2,1,0:T(8,128)S(1)} %copy-done), custom_call_target="tpu_custom_call" | custom-call | tf_op jit(solution)/shard_map/pallas_call | solution.py:278
  125.5 1.3 %copy.6 = bf16[1,512,2048]{2,1,0:T(8,128)(2,1)} copy(bf16[1,512,2048]{2,1,0:T(8,128)(2,1)S(1)} %bitcast.1) | data formatting | bytes 4194304
Async XLA Ops:
  0.6 0.7 copy-start.1
  119.1 2.2 %copy-start = (f32[8,64,2048]{2,1,0:T(8,128)S(1)}, f32[8,64,2048]{2,1,0:T(8,128)}, u32[]{:S(2)}) copy-start(f32[8,64,2048]{2,1,0:T(8,128)} %master_ref.1) | copy-start | bytes 12582916

commit v3 on v2

--- a/solution.py
+++ b/solution.py
@@ -32,10 +32,6 @@
     return lax.dot_general(
         left, right, (((1,), (1,)), ((), ())), preferred_element_type=jnp.float32
     )
-
-
-def far_first(count):
-    return sorted(range(1, count), key=lambda offset: (abs(2 * offset - count), -offset))
 
 
 def owner_kernel(
@@ -63,35 +59,70 @@
         pl.semaphore_signal(barrier, inc=1, device_id=(me, other), device_id_type=MESH)
     pl.semaphore_wait(barrier, n + 1)
 
-    def rows_in(offset, index):
+    quarter = n // 4
+    side = lax.div(me, 2 * quarter)
+
+    def owner(stage, index):
+        far = lax.rem(1 - side + index // quarter, 2)
+        base = quarter + quarter * far if stage == 0 else 3 * quarter * far
+        return base + lax.rem(me + index, quarter)
+
+    def for_owners(stage, body):
+        for index in range(2 * quarter):
+            dest = owner(stage, index)
+
+            @pl.when(dest != me)
+            def _():
+                body(stage * 2 * quarter + index, dest)
+
+    def rows_in(slot, dest, index):
         place = pl.ds(index * chunk, chunk)
         return pltpu.make_async_remote_copy(
-            src_ref=send.at[offset - 1, :, place],
+            src_ref=send.at[slot, :, place],
             dst_ref=recv.at[me, :, place],
-            send_sem=in_send.at[offset - 1, index],
-            recv_sem=in_recv.at[offset - 1, index],
-            device_id=(lax.rem(me + offset, n), lane),
+            send_sem=in_send.at[slot, index],
+            recv_sem=in_recv.at[me, index],
+            device_id=(dest, lane),
             device_id_type=MESH,
         )
 
-    for index in range(chunks):
-        for offset in far_first(n):
-            if index == 0:
-                send[offset - 1] = mom_ref[order_ref[lax.rem(me + offset, n)]]
-            rows_in(offset, index).start()
+    def fill(slot, dest):
+        send[slot] = mom_ref[order_ref[dest]]
+
+    def start_chunk(index):
+        return lambda slot, dest: rows_in(slot, dest, index).start()
+
+    def finish_chunk(index):
+        return lambda slot, dest: rows_in(slot, dest, index).wait_send()
+
+    def fill_and_start(slot, dest):
+        fill(slot, dest)
+        rows_in(slot, dest, 0).start()
+
+    for_owners(0, fill_and_start)
+    for index in range(1, chunks):
+        for_owners(0, start_chunk(index))
+    for_owners(1, fill)
     recv[me] = mom_ref[order_ref[me]]
+    for index in range(chunks - 1):
+        for_owners(0, finish_chunk(index))
+    for_owners(1, start_chunk(0))
+    for_owners(0, finish_chunk(chunks - 1))
+    for index in range(1, chunks):
+        for_owners(1, start_chunk(index))
 
     acc[...] = jnp.zeros_like(acc)
 
     def add_chunk(index, carry):
         place = pl.ds(pl.multiple_of(index * chunk, chunk), chunk)
         for offset in range(1, n):
+            source = lax.rem(me + offset, n)
             pltpu.make_async_remote_copy(
-                src_ref=send.at[offset - 1, :, place],
-                dst_ref=recv.at[lax.rem(me + n - offset, n), :, place],
-                send_sem=in_send.at[offset - 1, index],
-                recv_sem=in_recv.at[offset - 1, index],
-                device_id=(lax.rem(me + offset, n), lane),
+                src_ref=send.at[0, :, place],
+                dst_ref=recv.at[source, :, place],
+                send_sem=in_send.at[0, index],
+                recv_sem=in_recv.at[source, index],
+                device_id=(source, lane),
                 device_id_type=MESH,
             ).wait_recv()
         block = recv[:, :, place].reshape(size, chunk)
@@ -141,6 +172,13 @@
         scaled = gram[strip, :] * (inv_norm * inv_norm)
         acc[strip, :] = scaled
         gram_hi[strip, :], gram_lo[strip, :] = halves(scaled)
+
+    def joined(strip):
+        return (
+            narrow_dot(fac_hi[strip, :], all_hi[...])
+            + narrow_dot(fac_hi[strip, :], all_lo[...])
+            + narrow_dot(fac_lo[strip, :], all_hi[...])
+        )
 
     for step in range(ITERS):
         last = step + 1 == ITERS
@@ -162,19 +200,11 @@
                 following = narrow_dot(tmp_hi[strip, :], fac_hi[...])
                 acc[strip, :] = following
                 gram_hi[strip, :], gram_lo[strip, :] = halves(following)
-        if step > 0:
+        if step > 0 and not last:
             for start, strip in strips:
-                joined = (
-                    narrow_dot(fac_hi[strip, :], all_hi[...])
-                    + narrow_dot(fac_hi[strip, :], all_lo[...])
-                    + narrow_dot(fac_lo[strip, :], all_hi[...])
-                )
-                if last:
-                    joined = joined * (scale_out * inv_norm)
-                tmp_hi[strip, :], tmp_lo[strip, :] = halves(joined)
-            if not last:
-                all_hi[...] = tmp_hi[...]
-                all_lo[...] = tmp_lo[...]
+                tmp_hi[strip, :], tmp_lo[strip, :] = halves(joined(strip))
+            all_hi[...] = tmp_hi[...]
+            all_lo[...] = tmp_lo[...]
 
     def rows_out(dest):
         return pltpu.make_async_remote_copy(
@@ -186,27 +216,32 @@
             device_id_type=MESH,
         )
 
-    pairs = n // 2
+    pairs_side = n // 4
     pair = lax.div(me, 2)
     twin = me + 1 - 2 * lax.rem(me, 2)
-    for offset in far_first(pairs) + [0]:
-        first = 2 * lax.rem(pair + offset, pairs)
-        place = pl.ds(pl.multiple_of(first * rows, 2 * rows), 2 * rows)
-
-        def apply_chunk(index, carry):
-            lanes = pl.ds(pl.multiple_of(index * chunk, chunk), chunk)
-            block = recv[:, :, lanes].reshape(size, chunk)
-            upd[place, lanes] = (
-                narrow_dot(tmp_hi[place, :], block) + narrow_dot(tmp_lo[place, :], block)
-            ).astype(jnp.bfloat16)
-            return carry
-
-        lax.fori_loop(0, chunks, apply_chunk, 0)
-        if offset:
-            rows_out(first).start()
-            rows_out(first + 1).start()
-        else:
-            rows_out(twin).start()
+    for part in (0, 1):
+        target = 1 - side if part == 0 else side
+        strip = pl.ds(pl.multiple_of(target * half, half), half)
+        tmp_hi[strip, :], tmp_lo[strip, :] = halves(joined(strip) * (scale_out * inv_norm))
+        for index in range(pairs_side):
+            step = (index + part) % pairs_side
+            first = 2 * (target * pairs_side + lax.rem(pair + step, pairs_side))
+            place = pl.ds(pl.multiple_of(first * rows, 2 * rows), 2 * rows)
+
+            def apply_chunk(index, carry, place=place):
+                lanes = pl.ds(pl.multiple_of(index * chunk, chunk), chunk)
+                block = recv[:, :, lanes].reshape(size, chunk)
+                upd[place, lanes] = (
+                    narrow_dot(tmp_hi[place, :], block) + narrow_dot(tmp_lo[place, :], block)
+                ).astype(jnp.bfloat16)
+                return carry
+
+            lax.fori_loop(0, chunks, apply_chunk, 0)
+            if part == 1 and step == 0:
+                rows_out(twin).start()
+            else:
+                rows_out(first).start()
+                rows_out(first + 1).start()
     own = pltpu.make_async_copy(
         upd.at[pl.ds(pl.multiple_of(me * rows, rows), rows), :], ret_ref.at[me], local_sem.at[0]
     )
@@ -215,8 +250,7 @@
     whole.start()
 
     for index in range(chunks):
-        for offset in range(1, n):
-            rows_in(offset, index).wait_send()
+        for_owners(1, finish_chunk(index))
     own.wait()
     whole.wait()
     for offset in range(1, n):
@@ -252,45 +286,63 @@
         ],
         out_specs=(pl.BlockSpec(memory_space=pl.ANY), pl.BlockSpec(memory_space=pl.ANY)),
         scratch_shapes=[
-            pltpu.VMEM((n - 1, rows, cols), jnp.bfloat16),
+            pltpu.VMEM((n, rows, cols), jnp.bfloat16),
             pltpu.VMEM((n, rows, cols), jnp.bfloat16),
             pltpu.VMEM((size, cols), jnp.bfloat16),
             square_32, square_32, square_16, square_16, half_16, half_16,
             square_16, square_16, square_16, square_16, square_16, square_16, square_16, square_16,
-            dma((n - 1, 4)), dma((n - 1, 4)), dma((3,)), dma((3,)), dma((n,)), dma((n,)), dma((2,)),
+            dma((n, 4)), dma((n, 4)), dma((3,)), dma((3,)), dma((n,)), dma((n,)), dma((2,)),
         ],
         compiler_params=pltpu.CompilerParams(
-            collective_id=0, has_side_effects=True, vmem_limit_bytes=48 << 20
+            collective_id=0, has_side_effects=True, vmem_limit_bytes=30 << 20
+        ),
+        cost_estimate=pl.CostEstimate(
+            flops=6 * size * size * cols + 40 * size**3,
+            bytes_accessed=12 * size * cols,
+            transcendentals=0,
         ),
     )(owner_order, momentum)
 
 
-def master_kernel(order_ref, ret_ref, master_ref, out_ref):
-    out_ref[...] = master_ref[...] * (1.0 - learn_rate * weight_decay) - learn_rate * ret_ref[
-        ...
-    ].astype(jnp.float32)
-
-
-def master_call(returned, master, owner_order):
-    n, rows, cols = master.shape
-    by_slot = pl.BlockSpec((1, rows, cols), lambda slot, order: (slot, 0, 0))
-    by_matrix = pl.BlockSpec((1, rows, cols), lambda slot, order: (order[slot], 0, 0))
+def master_kernel(n, order_ref, ret_ref, upd_ref, master_ref, out_ref, upd_out_ref, fresh, sems):
+    whole = pltpu.make_async_copy(upd_ref, upd_out_ref, sems.at[n])
+    copies = []
+    for slot in range(n):
+        matrix = order_ref[slot]
+        fresh[slot] = master_ref[matrix] * (1.0 - learn_rate * weight_decay) - learn_rate * ret_ref[
+            slot
+        ].astype(jnp.float32)
+        copies.append(pltpu.make_async_copy(fresh.at[slot], out_ref.at[matrix], sems.at[slot]))
+        copies[-1].start()
+        if slot == 0:
+            whole.start()
+    for copy in copies + [whole]:
+        copy.wait()
+
+
+def master_call(returned, update, master, owner_order):
+    n = master.shape[0]
+    vmem = pl.BlockSpec(memory_space=pltpu.VMEM)
+    hbm = pl.BlockSpec(memory_space=pl.ANY)
     return pl.pallas_call(
-        master_kernel,
-        out_shape=jax.ShapeDtypeStruct(master.shape, jnp.float32),
-        grid_spec=pltpu.PrefetchScalarGridSpec(
-            num_scalar_prefetch=1,
-            grid=(n,),
-            in_specs=[by_slot, by_matrix],
-            out_specs=by_matrix,
+        functools.partial(master_kernel, n),
+        out_shape=(
+            jax.ShapeDtypeStruct(master.shape, jnp.float32),
+            jax.ShapeDtypeStruct(update.shape, update.dtype),
         ),
-        compiler_params=pltpu.CompilerParams(vmem_limit_bytes=32 << 20),
-    )(owner_order, returned, master)
+        in_specs=[pl.BlockSpec(memory_space=pltpu.SMEM), vmem, vmem, vmem],
+        out_specs=(hbm, hbm),
+        scratch_shapes=[
+            pltpu.VMEM(master.shape, jnp.float32), pltpu.SemaphoreType.DMA((n + 1,))
+        ],
+        compiler_params=pltpu.CompilerParams(vmem_limit_bytes=24 << 20),
+    )(owner_order, returned, update, master)
 
 
 def kernel_shards(scale_out, n, momentum, master, owner_order):
     returned, owned_update = owner_call(scale_out, n, momentum, owner_order)
-    return master_call(returned, master, owner_order), owned_update[None]
+    new_master, owned_update = master_call(returned, owned_update, master, owner_order)
+    return new_master, owned_update[None]
 
 
 def wide_dot(left, right):
@@ -345,7 +397,7 @@
 
         def shards(momentum, master, owner_order):
             matrices, rows, cols = momentum.shape
-            if matrices == n and lanes == 4 and rows % 16 == 0 and cols % 512 == 0:
+            if matrices == n and lanes == 4 and n % 4 == 0 and rows % 16 == 0 and cols % 512 == 0:
                 return kernel_shards(scale_out, n, momentum, master, owner_order)
             return plain_shards(scale_out, momentum, master, owner_order)
 

time: 127 us -> 133 us (1.047)
  the two profiles are of different devices: /device:TPU:13 before, /device:TPU:0 now
where the time goes in v3:
time: 133 us
  Pallas kernels  130 us (98%)
  local copies, waits for them, and re-layouts  2.24 us (2%)
    pallas_call x1, Pallas kernels, owner_call(): pl.pallas_call(functools.partial(owner_kernel, n, rows, cols, chunk, scal...  126 us
    pallas_call x1, Pallas kernels, master_call(): pl.pallas_call(functools.partial(master_kernel, n), out_shape=(jax.ShapeD...  3.34 us

profile of v3, /device:TPU:0, one launch (start us, length us, event | category | flops | bytes accessed | tf_op | source)
XLA Modules:
  0.0 132.6 jit_solution(10793681226575694420)
XLA Ops:
  0.6 0.0 copy-start.1
  0.6 0.6 copy-done.1
  1.3 0.0 copy-start.2
  1.3 1.6 %copy-done.2 = bf16[8,64,2048]{2,1,0:T(8,128)(2,1)S(1)} copy-done((bf16[8,64,2048]{2,1,0:T(8,128)(2,1)S(1)}, bf16[8,64,2048]{2,1,0:T(8,128)(2,1)}, u32[]{:S(2)}) %copy-start.2) | copy-done | bytes 2097176
  2.9 0.0 copy-start
  2.9 126.4 %shard_map.50 = (bf16[8,64,2048]{2,1,0:T(8,128)(2,1)S(1)}, bf16[512,2048]{1,0:T(8,128)(2,1)S(1)}) custom-call(s32[8]{0:T(128)S(1)} %copy-done.1, bf16[8,64,2048]{2,1,0:T(8,128)(2,1)S(1)} %copy-done.2), custom_call_target="tpu_custom_call" | custom-call | flops 8589934592 | bytes 12582912 | tf_op jit(solution)/shard_map/pallas_call | solution.py:277
  129.3 0.0 copy-done
  129.3 3.3 %shard_map.51 = (f32[8,64,2048]{2,1,0:T(8,128)}, bf16[512,2048]{1,0:T(8,128)(2,1)}) custom-call(s32[8]{0:T(128)S(1)} %copy-done.1, bf16[8,64,2048]{2,1,0:T(8,128)(2,1)S(1)} %get-tuple-element.6.ret_ref, bf16[512,2048]{1,0:T(8,128)(2,1)S(1)} %get-tuple-element.7.upd_ref, f32[8,64,2048]{2,1,0:T(8,128)S(1)} %copy-done), custom_call_target="tpu_custom_call" | custom-call | tf_op jit(solution)/shard_map/pallas_call | solution.py:327
Async XLA Ops:
  0.6 0.7 copy-start.1
  1.3 1.6 %copy-start.2 = (bf16[8,64,2048]{2,1,0:T(8,128)(2,1)S(1)}, bf16[8,64,2048]{2,1,0:T(8,128)(2,1)}, u32[]{:S(2)}) copy-start(bf16[8,64,2048]{2,1,0:T(8,128)(2,1)} %mom_ref.1) | copy-start | bytes 6291460
  2.9 126.4 %copy-start = (f32[8,64,2048]{2,1,0:T(8,128)S(1)}, f32[8,64,2048]{2,1,0:T(8,128)}, u32[]{:S(2)}) copy-start(f32[8,64,2048]{2,1,0:T(8,128)} %master_ref.1) | copy-start | bytes 12582916

commit v4 on v1

--- a/solution.py
+++ b/solution.py
@@ -1,8 +1,11 @@
+import functools
 import math
 
 import jax
 import jax.numpy as jnp
 from jax import lax
+from jax.experimental import pallas as pl
+from jax.experimental.pallas import tpu as pltpu
 from jax.sharding import PartitionSpec as P
 
 learn_rate = 0.02
@@ -12,6 +15,7 @@
 quintic_second = -4.775
 quintic_third = 2.0315
 ITERS = 3
+MESH = pl.DeviceIdType.MESH
 
 
 def halves(value):
@@ -24,24 +28,339 @@
     return jnp.dot(left, right, preferred_element_type=jnp.float32)
 
 
-def split_dot(left, right):
-    return (
-        narrow_dot(left[0], right[0]) + narrow_dot(left[0], right[1]) + narrow_dot(left[1], right[0])
+def transposed_dot(left, right):
+    return lax.dot_general(
+        left, right, (((1,), (1,)), ((), ())), preferred_element_type=jnp.float32
     )
 
 
+def visit_order(n):
+    last = [n - 2, 2]
+    near = [n - 1, 1]
+    rest = [offset for offset in range(1, n) if offset not in last + near]
+    return sorted(rest, key=lambda offset: (abs(offset - n // 2), offset)) + near + last
+
+
+def owner_kernel(
+    n, rows, cols, chunk, scale_out,
+    order_ref, mom_ref, ret_ref, upd_ref,
+    send, recv, upd, gram,
+    early, early_part, early_in, early_half, early_half_in, early_sum,
+    late, late_part, late_in, late_half, late_half_in, late_sum,
+    gram_left, gram_right, fac_left, all_right, passing, mixed,
+    in_send, in_recv, sum_send, sum_recv, out_send, out_recv, own_sem, write_sem,
+):
+    me = lax.axis_index("dp")
+    lane = lax.axis_index("tensor")
+    core = lax.rem(lane, 2)
+    mate = lane + 1 - 2 * core
+    across = lax.rem(lane + 2, 4)
+    size = n * rows
+    half = size // 2
+    first = size - 2 * rows
+    chunks = cols // chunk
+    order = visit_order(n)
+
+    barrier = pltpu.get_barrier_semaphore()
+    for offset in range(1, n):
+        pl.semaphore_signal(
+            barrier, inc=1, device_id=(lax.rem(me + offset, n), lane), device_id_type=MESH
+        )
+    for other in (mate, across):
+        pl.semaphore_signal(barrier, inc=1, device_id=(me, other), device_id_type=MESH)
+    pl.semaphore_wait(barrier, n + 1)
+
+    def rows_in(slot):
+        return pltpu.make_async_remote_copy(
+            src_ref=send.at[slot],
+            dst_ref=recv.at[slot],
+            send_sem=in_send.at[slot],
+            recv_sem=in_recv.at[slot],
+            device_id=(lax.rem(me + order[slot - 1], n), lane),
+            device_id_type=MESH,
+        )
+
+    def holder(slot):
+        return lax.rem(me + n - order[slot - 1], n) if slot else me
+
+    for slot in range(1, n):
+        send[slot] = mom_ref[order_ref[lax.rem(me + order[slot - 1], n)]]
+        rows_in(slot).start()
+    recv[0] = mom_ref[order_ref[me]]
+
+    def columns(index, start, count):
+        place = pl.ds(pl.multiple_of(index * chunk, chunk), chunk)
+        return recv[start : start + count, :, place].reshape(count * rows, chunk)
+
+    def tensor_sum(total, part, part_in, half_out, half_in, summed, sem):
+        count = total.shape[0] // 2
+        mine = pl.ds(pl.multiple_of(core * count, count), count)
+
+        def swap(step, source, target, other):
+            copy = pltpu.make_async_remote_copy(
+                src_ref=source, dst_ref=target,
+                send_sem=sum_send.at[sem + step], recv_sem=sum_recv.at[sem + step],
+                device_id=(me, other), device_id_type=MESH,
+            )
+            copy.start()
+            copy.wait()
+
+        part[...] = total[...].astype(jnp.bfloat16)
+        swap(0, part, part_in, mate)
+        half_out[...] = (
+            part[mine, :].astype(jnp.float32) + part_in[mine, :].astype(jnp.float32)
+        ).astype(jnp.bfloat16)
+        swap(1, half_out, half_in, across)
+        summed[mine, :] = half_out[...].astype(jnp.float32) + half_in[...].astype(jnp.float32)
+        swap(2, summed.at[mine, :], summed.at[mine, :], mate)
+
+    for slot in range(1, n - 2):
+        rows_in(slot).wait_recv()
+    early[...] = jnp.zeros_like(early)
+
+    def add_early(index, carry):
+        block = columns(index, 0, n - 2)
+        for start in (0, first // 2):
+            early[start : start + first // 2, :] += transposed_dot(
+                block[start : start + first // 2], block
+            )
+        return carry
+
+    lax.fori_loop(0, chunks, add_early, 0)
+    tensor_sum(early, early_part, early_in, early_half, early_half_in, early_sum, 0)
+
+    for slot in (n - 2, n - 1):
+        rows_in(slot).wait_recv()
+    late[...] = jnp.zeros_like(late)
+
+    def add_late(index, carry):
+        late[...] += transposed_dot(columns(index, n - 2, 2), columns(index, 0, n))
+        return carry
+
+    lax.fori_loop(0, chunks, add_late, 0)
+    tensor_sum(late, late_part, late_in, late_half, late_half_in, late_sum, 3)
+
+    def diagonal(height, width, start):
+        row = start + lax.broadcasted_iota(jnp.int32, (height, width), 0)
+        return row == lax.broadcasted_iota(jnp.int32, (height, width), 1)
+
+    def trace(value, start):
+        return jnp.sum(jnp.where(diagonal(*value.shape, start), value, 0.0), keepdims=True)
+
+    squares = trace(early_sum[...], 0) + trace(late_sum[...], first)
+    inv_norm = 1.0 / (jnp.sqrt(squares) + norm_epsilon)
+    square_scale = inv_norm * inv_norm
+    gram[:first, :first] = early_sum[...] * square_scale
+    gram[first:, :] = late_sum[...] * square_scale
+    gram[:first, first:] = late_sum[:, :first].T * square_scale
+
+    strips = [(start, slice(start, start + half)) for start in (0, half)]
+
+    def as_left(target, strip, value):
+        high, low = halves(value)
+        target[strip, 0:size] = high
+        target[strip, size : 2 * size] = high
+        target[strip, 2 * size :] = low
+
+    def as_right(target, start, value):
+        high, low = halves(value)
+        target[start : start + half, :] = high
+        target[size + start : size + start + half, :] = low
+        target[2 * size + start : 2 * size + start + half, :] = high
+
+    for start, strip in strips:
+        as_left(gram_left, strip, gram[strip, :])
+        as_right(gram_right, start, gram[strip, :])
+
+    for step in range(ITERS):
+        last = step + 1 == ITERS
+        for start, strip in strips:
+            factor = quintic_second * gram[strip, :] + quintic_third * narrow_dot(
+                gram_left[strip, :], gram_right[...]
+            )
+            factor += jnp.where(diagonal(half, size, start), quintic_first, 0.0)
+            as_left(fac_left, strip, factor)
+            if step == 0:
+                as_right(all_right, start, factor)
+        if not last:
+            for start, strip in strips:
+                mixed[strip, :] = narrow_dot(
+                    fac_left[strip, :size], gram_right[:size, :]
+                ).astype(jnp.bfloat16)
+            for start, strip in strips:
+                following = narrow_dot(mixed[strip, :], fac_left[:, :size])
+                gram[strip, :] = following
+                as_left(gram_left, strip, following)
+                as_right(gram_right, start, following)
+        if 0 < step and not last:
+            for start, strip in strips:
+                passing[strip, :] = narrow_dot(fac_left[strip, :], all_right[...])
+            for start, strip in strips:
+                as_right(all_right, start, passing[strip, :])
+
+    def rows_out(slot):
+        return pltpu.make_async_remote_copy(
+            src_ref=upd.at[slot * rows : (slot + 1) * rows, :],
+            dst_ref=ret_ref.at[me],
+            send_sem=out_send.at[slot],
+            recv_sem=out_recv.at[me],
+            device_id=(holder(slot), lane),
+            device_id_type=MESH,
+        )
+
+    def write(slot):
+        place = pl.ds(pl.multiple_of(holder(slot) * rows, rows), rows)
+        return pltpu.make_async_copy(
+            upd.at[slot * rows : (slot + 1) * rows, :], upd_ref.at[place, :], write_sem.at[slot]
+        )
+
+    own = pltpu.make_async_copy(upd.at[0:rows, :], ret_ref.at[me], own_sem.at[0])
+    for start, strip in strips:
+        high, low = halves(
+            narrow_dot(fac_left[strip, :], all_right[...]) * (scale_out * inv_norm)
+        )
+        mixed[strip, :] = high
+        fac_left[strip, :size] = low
+        for top in range(start, start + half, 2 * rows):
+
+            def apply_chunk(index, carry, top=top):
+                place = pl.ds(pl.multiple_of(index * chunk, chunk), chunk)
+                block = columns(index, 0, n)
+                upd[top : top + 2 * rows, place] = (
+                    narrow_dot(mixed[top : top + 2 * rows, :], block)
+                    + narrow_dot(fac_left[top : top + 2 * rows, :size], block)
+                ).astype(jnp.bfloat16)
+                return carry
+
+            lax.fori_loop(0, chunks, apply_chunk, 0)
+            for slot in (top // rows, top // rows + 1):
+                if slot:
+                    rows_out(slot).start()
+                else:
+                    own.start()
+    for slot in range(n):
+        write(slot).start()
+
+    for slot in range(1, n):
+        rows_in(slot).wait_send()
+    own.wait()
+    for slot in range(n):
+        write(slot).wait()
+    for slot in range(1, n):
+        rows_out(slot).wait_send()
+        source = lax.rem(me + slot, n)
+        pltpu.make_async_remote_copy(
+            src_ref=upd.at[0:rows, :],
+            dst_ref=ret_ref.at[source],
+            send_sem=out_send.at[slot],
+            recv_sem=out_recv.at[source],
+            device_id=(source, lane),
+            device_id_type=MESH,
+        ).wait_recv()
+
+
+def owner_call(scale_out, n, momentum, owner_order):
+    rows, cols = momentum.shape[1:]
+    size, first, strip = n * rows, (n - 2) * rows, 2 * rows
+
+    def wide(*shape):
+        return pltpu.VMEM(shape, jnp.float32)
+
+    def narrow(*shape):
+        return pltpu.VMEM(shape, jnp.bfloat16)
+
+    def gram_buffers(height, width):
+        return [
+            wide(height, width), narrow(height, width), narrow(height, width),
+            narrow(height // 2, width), narrow(height // 2, width), wide(height, width),
+        ]
+
+    dma = pltpu.SemaphoreType.DMA
+    return pl.pallas_call(
+        functools.partial(owner_kernel, n, rows, cols, cols // 4, scale_out),
+        out_shape=(
+            jax.ShapeDtypeStruct((n, rows, cols), jnp.bfloat16),
+            jax.ShapeDtypeStruct((size, cols), jnp.bfloat16),
+        ),
+        in_specs=[
+            pl.BlockSpec(memory_space=pltpu.SMEM),
+            pl.BlockSpec(memory_space=pltpu.VMEM),
+        ],
+        out_specs=(pl.BlockSpec(memory_space=pl.ANY), pl.BlockSpec(memory_space=pl.ANY)),
+        scratch_shapes=[
+            narrow(n, rows, cols), narrow(n, rows, cols), narrow(size, cols), wide(size, size),
+            *gram_buffers(first, first),
+            *gram_buffers(strip, size),
+            narrow(size, 3 * size), narrow(3 * size, size), narrow(size, 3 * size),
+            narrow(3 * size, size), wide(size, size), narrow(size, size),
+            dma((n,)), dma((n,)), dma((6,)), dma((6,)), dma((n,)), dma((n,)), dma((1,)), dma((n,)),
+        ],
+        compiler_params=pltpu.CompilerParams(
+            collective_id=0, has_side_effects=True, vmem_limit_bytes=32 << 20
+        ),
+        cost_estimate=pl.CostEstimate(
+            flops=6 * size * size * cols + 40 * size**3,
+            bytes_accessed=12 * size * cols,
+            transcendentals=0,
+        ),
+    )(owner_order, momentum)
+
+
+def master_kernel(n, order_ref, ret_ref, upd_ref, master_ref, out_ref, upd_out_ref, fresh, sems):
+    whole = pltpu.make_async_copy(upd_ref, upd_out_ref, sems.at[n])
+    copies = []
+    for slot in range(n):
+        matrix = order_ref[slot]
+        fresh[slot] = master_ref[matrix] * (1.0 - learn_rate * weight_decay) - learn_rate * ret_ref[
+            slot
+        ].astype(jnp.float32)
+        copies.append(pltpu.make_async_copy(fresh.at[slot], out_ref.at[matrix], sems.at[slot]))
+        copies[-1].start()
+        if slot == 0:
+            whole.start()
+    for copy in copies + [whole]:
+        copy.wait()
+
+
+def master_call(returned, update, master, owner_order):
+    n = master.shape[0]
+    vmem = pl.BlockSpec(memory_space=pltpu.VMEM)
+    hbm = pl.BlockSpec(memory_space=pl.ANY)
+    return pl.pallas_call(
+        functools.partial(master_kernel, n),
+        out_shape=(
+            jax.ShapeDtypeStruct(master.shape, jnp.float32),
+            jax.ShapeDtypeStruct(update.shape, update.dtype),
+        ),
+        in_specs=[pl.BlockSpec(memory_space=pltpu.SMEM), vmem, vmem, vmem],
+        out_specs=(hbm, hbm),
+        scratch_shapes=[
+            pltpu.VMEM(master.shape, jnp.float32), pltpu.SemaphoreType.DMA((n + 1,))
+        ],
+        compiler_params=pltpu.CompilerParams(vmem_limit_bytes=24 << 20),
+    )(owner_order, returned, update, master)
+
+
+def kernel_shards(scale_out, n, momentum, master, owner_order):
+    returned, owned_update = owner_call(scale_out, n, momentum, owner_order)
+    new_master, owned_update = master_call(returned, owned_update, master, owner_order)
+    return new_master, owned_update[None]
+
+
+def wide_dot(left, right):
+    return jnp.dot(left, right, precision=lax.Precision.HIGH)
+
+
 def polynomial(gram):
-    size = gram.shape[0]
-    eye = jnp.eye(size, dtype=jnp.float32)
+    eye = jnp.eye(gram.shape[0], dtype=jnp.float32)
     whole = None
     for step in range(ITERS):
-        gram_halves = halves(gram)
-        square = split_dot(gram_halves, gram_halves)
-        factor = quintic_first * eye + quintic_second * gram + quintic_third * square
-        factor_halves = halves(factor)
-        whole = factor if whole is None else split_dot(factor_halves, halves(whole))
+        factor = (
+            quintic_first * eye + quintic_second * gram + quintic_third * wide_dot(gram, gram)
+        )
+        whole = factor if whole is None else wide_dot(factor, whole)
         if step + 1 < ITERS:
-            gram = split_dot(halves(split_dot(factor_halves, gram_halves)), factor_halves)
+            gram = wide_dot(wide_dot(factor, gram), factor)
     return whole
 
 
@@ -58,8 +377,7 @@
         )
         gram = lax.psum(partial_value.astype(jnp.bfloat16), "tensor").astype(jnp.float32)
         whole = polynomial(gram * (inv_norm * inv_norm)) * (scale_out * inv_norm)
-        high, low = halves(whole)
-        return (narrow_dot(high, matrix) + narrow_dot(low, matrix)).astype(jnp.bfloat16)
+        return wide_dot(whole, matrix.astype(jnp.float32)).astype(jnp.bfloat16)
 
     owned_update = jnp.stack([one(owned[index]) for index in range(owned.shape[0])])
     returned = lax.all_to_all(owned_update, "dp", split_axis=1, concat_axis=0, tiled=True)
@@ -74,10 +392,15 @@
 
 
 def solution(mesh):
+    n, lanes = mesh.shape["dp"], mesh.shape["tensor"]
+
     def whole_call(momentum, master, owner_order):
         scale_out = 0.2 * math.sqrt(max(momentum.shape[1], momentum.shape[2]))
 
         def shards(momentum, master, owner_order):
+            matrices, rows, cols = momentum.shape
+            if matrices == n and lanes == 4 and n >= 8 and n % 4 == 0 and rows % 64 == 0 and cols % 512 == 0:
+                return kernel_shards(scale_out, n, momentum, master, owner_order)
             return plain_shards(scale_out, momentum, master, owner_order)
 
         return jax.shard_map(

time: 218 us -> 122 us (0.56)
  Pallas kernels: 0 us -> 117 us
  waiting for transfers between devices: 70.3 us -> 0 us
  blocking collectives: 61.6 us -> 0 us
  other arithmetic: 24.3 us -> 0 us
  local copies, waits for them, and re-layouts: 22.4 us -> 2.24 us
  matrix products: 18.3 us -> 0 us
  between operations: 15 us -> 0.66 us
  starting transfers between devices: 5.55 us -> 0 us
    pallas_call x0 -> x2, Pallas kernels: none -> 117 us  [the longest x1 113 us: owner_call(): pl.pallas_call(functools.partial(owner_kernel, n, rows, cols, cols // 4,...]
    all_to_all x1 -> x0, blocking collectives: 55.3 us -> none  [plain_shards(): lax.all_to_all(slotted, 'dp', split_axis=0, concat_axis=1, tiled=True)]
    all_to_all x1 -> x0, waiting for transfers between devices: 46.7 us -> none  [plain_shards(): lax.all_to_all(owned_update, 'dp', split_axis=1, concat_axis=0, tiled=True)]
    psum x1 -> x0, waiting for transfers between devices: 23.6 us -> none  [one(): lax.psum(partial_value.astype(jnp.bfloat16), 'tensor').astype(jnp.float32)]
    dot_general x30 -> x0, matrix products: 18.3 us -> none  [the longest x29 16.3 us: narrow_dot(): return jnp.dot(left, right, preferred_element_type=jnp.float32)]
    unnamed x1 -> x0, other arithmetic: 13.2 us -> none
    unnamed x12 -> x6, local copies, waits for them, and re-layouts: 12.3 us -> 2.24 us
    psum x1 -> x0, blocking collectives: 6.27 us -> none  [one(): lax.psum(jnp.sum(jnp.square(matrix.astype(jnp.float32))), 'tensor')]
  transfers between devices with their start and end apart: 2 -> 0, of which waited for: 2 -> 0; matrix products, arithmetic and copies ran while one was open for 1% -> 0% of each run, Pallas kernels for 0% -> 0%
where the time goes in v4:
time: 122 us; the launch traced here: 120 us
  Pallas kernels  117 us (96%)
  local copies, waits for them, and re-layouts  2.24 us (2%)
    pallas_call x1, Pallas kernels, owner_call(): pl.pallas_call(functools.partial(owner_kernel, n, rows, cols, cols // 4,...  113 us
    pallas_call x1, Pallas kernels, master_call(): pl.pallas_call(functools.partial(master_kernel, n), out_shape=(jax.ShapeD...  3.34 us

profile of v4, /device:TPU:0, one launch (start us, length us, event | category | flops | bytes accessed | tf_op | source)
XLA Modules:
  0.0 119.6 jit_solution(6150106693479845529)
XLA Ops:
  0.6 0.0 copy-start.1
  0.6 0.6 copy-done.1
  1.3 0.0 copy-start.2
  1.3 1.6 %copy-done.2 = bf16[8,64,2048]{2,1,0:T(8,128)(2,1)S(1)} copy-done((bf16[8,64,2048]{2,1,0:T(8,128)(2,1)S(1)}, bf16[8,64,2048]{2,1,0:T(8,128)(2,1)}, u32[]{:S(2)}) %copy-start.2) | copy-done | bytes 2097176
  2.9 0.0 copy-start
  2.9 113.3 %shard_map.50 = (bf16[8,64,2048]{2,1,0:T(8,128)(2,1)S(1)}, bf16[512,2048]{1,0:T(8,128)(2,1)S(1)}) custom-call(s32[8]{0:T(128)S(1)} %copy-done.1, bf16[8,64,2048]{2,1,0:T(8,128)(2,1)S(1)} %copy-done.2), custom_call_target="tpu_custom_call" | custom-call | flops 8589934592 | bytes 12582912 | tf_op jit(solution)/shard_map/pallas_call | solution.py:279
  116.2 0.0 copy-done
  116.2 3.3 %shard_map.51 = (f32[8,64,2048]{2,1,0:T(8,128)}, bf16[512,2048]{1,0:T(8,128)(2,1)}) custom-call(s32[8]{0:T(128)S(1)} %copy-done.1, bf16[8,64,2048]{2,1,0:T(8,128)(2,1)S(1)} %get-tuple-element.6.ret_ref, bf16[512,2048]{1,0:T(8,128)(2,1)S(1)} %get-tuple-element.7.upd_ref, f32[8,64,2048]{2,1,0:T(8,128)S(1)} %copy-done), custom_call_target="tpu_custom_call" | custom-call | tf_op jit(solution)/shard_map/pallas_call | solution.py:329
Async XLA Ops:
  0.6 0.7 copy-start.1
  1.3 1.6 %copy-start.2 = (bf16[8,64,2048]{2,1,0:T(8,128)(2,1)S(1)}, bf16[8,64,2048]{2,1,0:T(8,128)(2,1)}, u32[]{:S(2)}) copy-start(bf16[8,64,2048]{2,1,0:T(8,128)(2,1)} %mom_ref.1) | copy-start | bytes 6291460
  2.9 113.3 %copy-start = (f32[8,64,2048]{2,1,0:T(8,128)S(1)}, f32[8,64,2048]{2,1,0:T(8,128)}, u32[]{:S(2)}) copy-start(f32[8,64,2048]{2,1,0:T(8,128)} %master_ref.1) | copy-start | bytes 12582916

commit v5 on v4

--- a/solution.py
+++ b/solution.py
@@ -36,9 +36,11 @@
 
 def visit_order(n):
     last = [n - 2, 2]
-    near = [n - 1, 1]
-    rest = [offset for offset in range(1, n) if offset not in last + near]
-    return sorted(rest, key=lambda offset: (abs(offset - n // 2), offset)) + near + last
+    rest = [offset for offset in range(1, n) if offset not in last]
+    rest.sort(key=lambda offset: (abs(offset - n // 2), offset))
+    count = len(rest)
+    mixed = [rest[index // 2 if index % 2 == 0 else count - 1 - index // 2] for index in range(count)]
+    return mixed + last
 
 
 def owner_kernel(
@@ -70,12 +72,15 @@
         pl.semaphore_signal(barrier, inc=1, device_id=(me, other), device_id_type=MESH)
     pl.semaphore_wait(barrier, n + 1)
 
-    def rows_in(slot):
+    def lanes_of(index):
+        return pl.ds(pl.multiple_of(index * chunk, chunk), chunk)
+
+    def rows_in(slot, index):
         return pltpu.make_async_remote_copy(
-            src_ref=send.at[slot],
-            dst_ref=recv.at[slot],
-            send_sem=in_send.at[slot],
-            recv_sem=in_recv.at[slot],
+            src_ref=send.at[slot, :, lanes_of(index)],
+            dst_ref=recv.at[slot, :, lanes_of(index)],
+            send_sem=in_send.at[slot, index],
+            recv_sem=in_recv.at[slot, index],
             device_id=(lax.rem(me + order[slot - 1], n), lane),
             device_id_type=MESH,
         )
@@ -83,14 +88,16 @@
     def holder(slot):
         return lax.rem(me + n - order[slot - 1], n) if slot else me
 
-    for slot in range(1, n):
-        send[slot] = mom_ref[order_ref[lax.rem(me + order[slot - 1], n)]]
-        rows_in(slot).start()
+    for slots in (range(1, n - 2), range(n - 2, n)):
+        for index in range(chunks):
+            for slot in slots:
+                if index == 0:
+                    send[slot] = mom_ref[order_ref[lax.rem(me + order[slot - 1], n)]]
+                rows_in(slot, index).start()
     recv[0] = mom_ref[order_ref[me]]
 
     def columns(index, start, count):
-        place = pl.ds(pl.multiple_of(index * chunk, chunk), chunk)
-        return recv[start : start + count, :, place].reshape(count * rows, chunk)
+        return recv[start : start + count, :, lanes_of(index)].reshape(count * rows, chunk)
 
     def tensor_sum(total, part, part_in, half_out, half_in, summed, sem):
         count = total.shape[0] // 2
@@ -114,11 +121,11 @@
         summed[mine, :] = half_out[...].astype(jnp.float32) + half_in[...].astype(jnp.float32)
         swap(2, summed.at[mine, :], summed.at[mine, :], mate)
 
-    for slot in range(1, n - 2):
-        rows_in(slot).wait_recv()
     early[...] = jnp.zeros_like(early)
 
     def add_early(index, carry):
+        for slot in range(1, n - 2):
+            rows_in(slot, index).wait_recv()
         block = columns(index, 0, n - 2)
         for start in (0, first // 2):
             early[start : start + first // 2, :] += transposed_dot(
@@ -129,11 +136,11 @@
     lax.fori_loop(0, chunks, add_early, 0)
     tensor_sum(early, early_part, early_in, early_half, early_half_in, early_sum, 0)
 
-    for slot in (n - 2, n - 1):
-        rows_in(slot).wait_recv()
     late[...] = jnp.zeros_like(late)
 
     def add_late(index, carry):
+        for slot in (n - 2, n - 1):
+            rows_in(slot, index).wait_recv()
         late[...] += transposed_dot(columns(index, n - 2, 2), columns(index, 0, n))
         return carry
 
@@ -198,12 +205,12 @@
             for start, strip in strips:
                 as_right(all_right, start, passing[strip, :])
 
-    def rows_out(slot):
+    def rows_out(slot, index):
         return pltpu.make_async_remote_copy(
-            src_ref=upd.at[slot * rows : (slot + 1) * rows, :],
-            dst_ref=ret_ref.at[me],
-            send_sem=out_send.at[slot],
-            recv_sem=out_recv.at[me],
+            src_ref=upd.at[slot * rows : (slot + 1) * rows, lanes_of(index)],
+            dst_ref=ret_ref.at[me, :, lanes_of(index)],
+            send_sem=out_send.at[slot, index],
+            recv_sem=out_recv.at[me, index],
             device_id=(holder(slot), lane),
             device_id_type=MESH,
         )
@@ -214,49 +221,48 @@
             upd.at[slot * rows : (slot + 1) * rows, :], upd_ref.at[place, :], write_sem.at[slot]
         )
 
-    own = pltpu.make_async_copy(upd.at[0:rows, :], ret_ref.at[me], own_sem.at[0])
     for start, strip in strips:
         high, low = halves(
             narrow_dot(fac_left[strip, :], all_right[...]) * (scale_out * inv_norm)
         )
         mixed[strip, :] = high
         fac_left[strip, :size] = low
-        for top in range(start, start + half, 2 * rows):
-
-            def apply_chunk(index, carry, top=top):
-                place = pl.ds(pl.multiple_of(index * chunk, chunk), chunk)
-                block = columns(index, 0, n)
-                upd[top : top + 2 * rows, place] = (
-                    narrow_dot(mixed[top : top + 2 * rows, :], block)
-                    + narrow_dot(fac_left[top : top + 2 * rows, :size], block)
-                ).astype(jnp.bfloat16)
-                return carry
-
-            lax.fori_loop(0, chunks, apply_chunk, 0)
-            for slot in (top // rows, top // rows + 1):
+
+    def apply_chunk(index, carry):
+        block = columns(index, 0, n)
+        for start, strip in strips:
+            upd[strip, lanes_of(index)] = (
+                narrow_dot(mixed[strip, :], block) + narrow_dot(fac_left[strip, :size], block)
+            ).astype(jnp.bfloat16)
+            for slot in range(start // rows, (start + half) // rows):
                 if slot:
-                    rows_out(slot).start()
-                else:
-                    own.start()
+                    rows_out(slot, index).start()
+        return carry
+
+    lax.fori_loop(0, chunks, apply_chunk, 0)
+    own = pltpu.make_async_copy(upd.at[0:rows, :], ret_ref.at[me], own_sem.at[0])
+    own.start()
     for slot in range(n):
         write(slot).start()
 
     for slot in range(1, n):
-        rows_in(slot).wait_send()
+        for index in range(chunks):
+            rows_in(slot, index).wait_send()
     own.wait()
     for slot in range(n):
         write(slot).wait()
     for slot in range(1, n):
-        rows_out(slot).wait_send()
         source = lax.rem(me + slot, n)
-        pltpu.make_async_remote_copy(
-            src_ref=upd.at[0:rows, :],
-            dst_ref=ret_ref.at[source],
-            send_sem=out_send.at[slot],
-            recv_sem=out_recv.at[source],
-            device_id=(source, lane),
-            device_id_type=MESH,
-        ).wait_recv()
+        for index in range(chunks):
+            rows_out(slot, index).wait_send()
+            pltpu.make_async_remote_copy(
+                src_ref=upd.at[0:rows, lanes_of(index)],
+                dst_ref=ret_ref.at[source, :, lanes_of(index)],
+                send_sem=out_send.at[slot, index],
+                recv_sem=out_recv.at[source, index],
+                device_id=(source, lane),
+                device_id_type=MESH,
+            ).wait_recv()
 
 
 def owner_call(scale_out, n, momentum, owner_order):
@@ -293,7 +299,8 @@
             *gram_buffers(strip, size),
             narrow(size, 3 * size), narrow(3 * size, size), narrow(size, 3 * size),
             narrow(3 * size, size), wide(size, size), narrow(size, size),
-            dma((n,)), dma((n,)), dma((6,)), dma((6,)), dma((n,)), dma((n,)), dma((1,)), dma((n,)),
+            dma((n, 4)), dma((n, 4)), dma((6,)), dma((6,)),
+            dma((n, 4)), dma((n, 4)), dma((1,)), dma((n,)),
         ],
         compiler_params=pltpu.CompilerParams(
             collective_id=0, has_side_effects=True, vmem_limit_bytes=32 << 20

time: 122 us -> 123 us (level); the launches traced: 120 us -> 123 us
  Pallas kernels: 117 us -> 120 us
    pallas_call x1, Pallas kernels: 113 us -> 117 us  [owner_call(): pl.pallas_call(functools.partial(owner_kernel, n, rows, cols, cols // 4,...]
where the time goes in v5:
time: 123 us
  Pallas kernels  120 us (98%)
  local copies, waits for them, and re-layouts  2.24 us (2%)
    pallas_call x1, Pallas kernels, owner_call(): pl.pallas_call(functools.partial(owner_kernel, n, rows, cols, cols // 4,...  117 us
    pallas_call x1, Pallas kernels, master_call(): pl.pallas_call(functools.partial(master_kernel, n), out_shape=(jax.ShapeD...  3.34 us

profile of v5, /device:TPU:0, one launch (start us, length us, event | category | flops | bytes accessed | tf_op | source)
XLA Modules:
  0.0 123.2 jit_solution(11036589189199600745)
XLA Ops:
  0.6 0.0 copy-start.1
  0.6 0.6 copy-done.1
  1.3 0.0 copy-start.2
  1.3 1.6 %copy-done.2 = bf16[8,64,2048]{2,1,0:T(8,128)(2,1)S(1)} copy-done((bf16[8,64,2048]{2,1,0:T(8,128)(2,1)S(1)}, bf16[8,64,2048]{2,1,0:T(8,128)(2,1)}, u32[]{:S(2)}) %copy-start.2) | copy-done | bytes 2097176
  2.9 0.0 copy-start
  2.9 117.0 %shard_map.50 = (bf16[8,64,2048]{2,1,0:T(8,128)(2,1)S(1)}, bf16[512,2048]{1,0:T(8,128)(2,1)S(1)}) custom-call(s32[8]{0:T(128)S(1)} %copy-done.1, bf16[8,64,2048]{2,1,0:T(8,128)(2,1)S(1)} %copy-done.2), custom_call_target="tpu_custom_call" | custom-call | flops 8589934592 | bytes 12582912 | tf_op jit(solution)/shard_map/pallas_call | solution.py:285
  119.8 0.0 copy-done
  119.8 3.3 %shard_map.51 = (f32[8,64,2048]{2,1,0:T(8,128)}, bf16[512,2048]{1,0:T(8,128)(2,1)}) custom-call(s32[8]{0:T(128)S(1)} %copy-done.1, bf16[8,64,2048]{2,1,0:T(8,128)(2,1)S(1)} %get-tuple-element.6.ret_ref, bf16[512,2048]{1,0:T(8,128)(2,1)S(1)} %get-tuple-element.7.upd_ref, f32[8,64,2048]{2,1,0:T(8,128)S(1)} %copy-done), custom_call_target="tpu_custom_call" | custom-call | tf_op jit(solution)/shard_map/pallas_call | solution.py:336
Async XLA Ops:
  0.6 0.7 copy-start.1
  1.3 1.6 %copy-start.2 = (bf16[8,64,2048]{2,1,0:T(8,128)(2,1)S(1)}, bf16[8,64,2048]{2,1,0:T(8,128)(2,1)}, u32[]{:S(2)}) copy-start(bf16[8,64,2048]{2,1,0:T(8,128)(2,1)} %mom_ref.1) | copy-start | bytes 6291460
  2.9 117.0 %copy-start = (f32[8,64,2048]{2,1,0:T(8,128)S(1)}, f32[8,64,2048]{2,1,0:T(8,128)}, u32[]{:S(2)}) copy-start(f32[8,64,2048]{2,1,0:T(8,128)} %master_ref.1) | copy-start | bytes 12582916

commit v6 on v4

--- a/solution.py
+++ b/solution.py
@@ -47,7 +47,7 @@
     send, recv, upd, gram,
     early, early_part, early_in, early_half, early_half_in, early_sum,
     late, late_part, late_in, late_half, late_half_in, late_sum,
-    gram_left, gram_right, fac_left, all_right, passing, mixed,
+    mixed, fac, fac_first, pair_hi, pair_lo, whole_hi, whole_lo,
     in_send, in_recv, sum_send, sum_recv, out_send, out_recv, own_sem, write_sem,
 ):
     me = lax.axis_index("dp")
@@ -150,53 +150,29 @@
     squares = trace(early_sum[...], 0) + trace(late_sum[...], first)
     inv_norm = 1.0 / (jnp.sqrt(squares) + norm_epsilon)
     square_scale = inv_norm * inv_norm
-    gram[:first, :first] = early_sum[...] * square_scale
-    gram[first:, :] = late_sum[...] * square_scale
-    gram[:first, first:] = late_sum[:, :first].T * square_scale
+    gram[:first, :first] = (early_sum[...] * square_scale).astype(jnp.bfloat16)
+    gram[first:, :] = (late_sum[...] * square_scale).astype(jnp.bfloat16)
+    gram[:first, first:] = (late_sum[:, :first].T * square_scale).astype(jnp.bfloat16)
 
     strips = [(start, slice(start, start + half)) for start in (0, half)]
-
-    def as_left(target, strip, value):
-        high, low = halves(value)
-        target[strip, 0:size] = high
-        target[strip, size : 2 * size] = high
-        target[strip, 2 * size :] = low
-
-    def as_right(target, start, value):
-        high, low = halves(value)
-        target[start : start + half, :] = high
-        target[size + start : size + start + half, :] = low
-        target[2 * size + start : 2 * size + start + half, :] = high
-
-    for start, strip in strips:
-        as_left(gram_left, strip, gram[strip, :])
-        as_right(gram_right, start, gram[strip, :])
-
     for step in range(ITERS):
-        last = step + 1 == ITERS
         for start, strip in strips:
-            factor = quintic_second * gram[strip, :] + quintic_third * narrow_dot(
-                gram_left[strip, :], gram_right[...]
-            )
+            factor = quintic_second * gram[strip, :].astype(jnp.float32)
+            factor += quintic_third * narrow_dot(gram[strip, :], gram[...])
             factor += jnp.where(diagonal(half, size, start), quintic_first, 0.0)
-            as_left(fac_left, strip, factor)
-            if step == 0:
-                as_right(all_right, start, factor)
-        if not last:
+            fac[strip, :] = factor.astype(jnp.bfloat16)
+        if step + 1 < ITERS:
             for start, strip in strips:
-                mixed[strip, :] = narrow_dot(
-                    fac_left[strip, :size], gram_right[:size, :]
-                ).astype(jnp.bfloat16)
+                mixed[strip, :] = narrow_dot(fac[strip, :], gram[...]).astype(jnp.bfloat16)
             for start, strip in strips:
-                following = narrow_dot(mixed[strip, :], fac_left[:, :size])
-                gram[strip, :] = following
-                as_left(gram_left, strip, following)
-                as_right(gram_right, start, following)
-        if 0 < step and not last:
+                gram[strip, :] = narrow_dot(mixed[strip, :], fac[...]).astype(jnp.bfloat16)
+        if step == 0:
+            fac_first[...] = fac[...]
+        elif step == 1:
             for start, strip in strips:
-                passing[strip, :] = narrow_dot(fac_left[strip, :], all_right[...])
-            for start, strip in strips:
-                as_right(all_right, start, passing[strip, :])
+                pair_hi[strip, :], pair_lo[strip, :] = halves(
+                    narrow_dot(fac[strip, :], fac_first[...])
+                )
 
     def rows_out(slot):
         return pltpu.make_async_remote_copy(
@@ -217,18 +193,19 @@
     own = pltpu.make_async_copy(upd.at[0:rows, :], ret_ref.at[me], own_sem.at[0])
     for start, strip in strips:
         high, low = halves(
-            narrow_dot(fac_left[strip, :], all_right[...]) * (scale_out * inv_norm)
-        )
-        mixed[strip, :] = high
-        fac_left[strip, :size] = low
+            (narrow_dot(fac[strip, :], pair_hi[...]) + narrow_dot(fac[strip, :], pair_lo[...]))
+            * (scale_out * inv_norm)
+        )
+        whole_hi[strip, :] = high
+        whole_lo[strip, :] = low
         for top in range(start, start + half, 2 * rows):
 
             def apply_chunk(index, carry, top=top):
                 place = pl.ds(pl.multiple_of(index * chunk, chunk), chunk)
                 block = columns(index, 0, n)
                 upd[top : top + 2 * rows, place] = (
-                    narrow_dot(mixed[top : top + 2 * rows, :], block)
-                    + narrow_dot(fac_left[top : top + 2 * rows, :size], block)
+                    narrow_dot(whole_hi[top : top + 2 * rows, :], block)
+                    + narrow_dot(whole_lo[top : top + 2 * rows, :], block)
                 ).astype(jnp.bfloat16)
                 return carry
 
@@ -288,11 +265,10 @@
         ],
         out_specs=(pl.BlockSpec(memory_space=pl.ANY), pl.BlockSpec(memory_space=pl.ANY)),
         scratch_shapes=[
-            narrow(n, rows, cols), narrow(n, rows, cols), narrow(size, cols), wide(size, size),
+            narrow(n, rows, cols), narrow(n, rows, cols), narrow(size, cols), narrow(size, size),
             *gram_buffers(first, first),
             *gram_buffers(strip, size),
-            narrow(size, 3 * size), narrow(3 * size, size), narrow(size, 3 * size),
-            narrow(3 * size, size), wide(size, size), narrow(size, size),
+            *[narrow(size, size)] * 7,
             dma((n,)), dma((n,)), dma((6,)), dma((6,)), dma((n,)), dma((n,)), dma((1,)), dma((n,)),
         ],
         compiler_params=pltpu.CompilerParams(

time: 122 us -> 119 us (0.975)
  Pallas kernels: 117 us -> 114 us
    pallas_call x1, Pallas kernels: 113 us -> 111 us  [owner_call(): pl.pallas_call(functools.partial(owner_kernel, n, rows, cols, cols // 4,...]
where the time goes in v6:
time: 119 us; the launch traced here: 117 us
  Pallas kernels  114 us (96%)
  local copies, waits for them, and re-layouts  2.24 us (2%)
    pallas_call x1, Pallas kernels, owner_call(): pl.pallas_call(functools.partial(owner_kernel, n, rows, cols, cols // 4,...  111 us
    pallas_call x1, Pallas kernels, master_call(): pl.pallas_call(functools.partial(master_kernel, n), out_shape=(jax.ShapeD...  3.34 us

profile of v6, /device:TPU:0, one launch (start us, length us, event | category | flops | bytes accessed | tf_op | source)
XLA Modules:
  0.0 117.2 jit_solution(12912541100767482713)
XLA Ops:
  0.6 0.0 copy-start.1
  0.6 0.6 copy-done.1
  1.3 0.0 copy-start.2
  1.3 1.6 %copy-done.2 = bf16[8,64,2048]{2,1,0:T(8,128)(2,1)S(1)} copy-done((bf16[8,64,2048]{2,1,0:T(8,128)(2,1)S(1)}, bf16[8,64,2048]{2,1,0:T(8,128)(2,1)}, u32[]{:S(2)}) %copy-start.2) | copy-done | bytes 2097176
  2.9 0.0 copy-start
  2.9 111.0 %shard_map.50 = (bf16[8,64,2048]{2,1,0:T(8,128)(2,1)S(1)}, bf16[512,2048]{1,0:T(8,128)(2,1)S(1)}) custom-call(s32[8]{0:T(128)S(1)} %copy-done.1, bf16[8,64,2048]{2,1,0:T(8,128)(2,1)S(1)} %copy-done.2), custom_call_target="tpu_custom_call" | custom-call | flops 8589934592 | bytes 12582912 | tf_op jit(solution)/shard_map/pallas_call | solution.py:256
  113.9 0.0 copy-done
  113.9 3.3 %shard_map.51 = (f32[8,64,2048]{2,1,0:T(8,128)}, bf16[512,2048]{1,0:T(8,128)(2,1)}) custom-call(s32[8]{0:T(128)S(1)} %copy-done.1, bf16[8,64,2048]{2,1,0:T(8,128)(2,1)S(1)} %get-tuple-element.6.ret_ref, bf16[512,2048]{1,0:T(8,128)(2,1)S(1)} %get-tuple-element.7.upd_ref, f32[8,64,2048]{2,1,0:T(8,128)S(1)} %copy-done), custom_call_target="tpu_custom_call" | custom-call | tf_op jit(solution)/shard_map/pallas_call | solution.py:305
Async XLA Ops:
  0.6 0.7 copy-start.1
  1.3 1.6 %copy-start.2 = (bf16[8,64,2048]{2,1,0:T(8,128)(2,1)S(1)}, bf16[8,64,2048]{2,1,0:T(8,128)(2,1)}, u32[]{:S(2)}) copy-start(bf16[8,64,2048]{2,1,0:T(8,128)(2,1)} %mom_ref.1) | copy-start | bytes 6291460
  2.9 111.0 %copy-start = (f32[8,64,2048]{2,1,0:T(8,128)S(1)}, f32[8,64,2048]{2,1,0:T(8,128)}, u32[]{:S(2)}) copy-start(f32[8,64,2048]{2,1,0:T(8,128)} %master_ref.1) | copy-start | bytes 12582916

commit v7 on v6

--- a/solution.py
+++ b/solution.py
@@ -34,11 +34,9 @@
     )
 
 
-def visit_order(n):
-    last = [n - 2, 2]
-    near = [n - 1, 1]
-    rest = [offset for offset in range(1, n) if offset not in last + near]
-    return sorted(rest, key=lambda offset: (abs(offset - n // 2), offset)) + near + last
+def visit_shifts(n):
+    shifts = [(pair, bit) for pair in range(1, n // 2) for bit in (0, 1)]
+    return shifts[:2] + [(0, 1)] + shifts[2:]
 
 
 def owner_kernel(
@@ -59,7 +57,29 @@
     half = size // 2
     first = size - 2 * rows
     chunks = cols // chunk
-    order = visit_order(n)
+    shifts = visit_shifts(n)
+    pairs = n // 2
+    pair = lax.div(me, 2)
+    bit = lax.rem(me, 2)
+    even = lax.rem(pair, 2) == 0
+
+    def target(slot):
+        shift = shifts[slot - 1]
+        return 2 * lax.rem(pair + shift[0], pairs) + lax.rem(bit + shift[1], 2)
+
+    def holder(slot):
+        if slot == 0:
+            return me
+        shift = shifts[slot - 1]
+        return 2 * lax.rem(pair + pairs - shift[0], pairs) + lax.rem(bit + shift[1], 2)
+
+    def start_in_turn(slot, start):
+        if slot == 3:
+            pl.when(even)(lambda: start(3))
+        else:
+            start(slot)
+        if slot == 5:
+            pl.when(jnp.logical_not(even))(lambda: start(3))
 
     barrier = pltpu.get_barrier_semaphore()
     for offset in range(1, n):
@@ -76,16 +96,13 @@
             dst_ref=recv.at[slot],
             send_sem=in_send.at[slot],
             recv_sem=in_recv.at[slot],
-            device_id=(lax.rem(me + order[slot - 1], n), lane),
+            device_id=(target(slot), lane),
             device_id_type=MESH,
         )
 
-    def holder(slot):
-        return lax.rem(me + n - order[slot - 1], n) if slot else me
-
     for slot in range(1, n):
-        send[slot] = mom_ref[order_ref[lax.rem(me + order[slot - 1], n)]]
-        rows_in(slot).start()
+        send[slot] = mom_ref[order_ref[target(slot)]]
+        start_in_turn(slot, lambda slot: rows_in(slot).start())
     recv[0] = mom_ref[order_ref[me]]
 
     def columns(index, start, count):
@@ -212,7 +229,7 @@
             lax.fori_loop(0, chunks, apply_chunk, 0)
             for slot in (top // rows, top // rows + 1):
                 if slot:
-                    rows_out(slot).start()
+                    start_in_turn(slot, lambda slot: rows_out(slot).start())
                 else:
                     own.start()
     for slot in range(n):

time: 119 us -> 126 us (1.059); the launches traced: 117 us -> 126 us
  Pallas kernels: 114 us -> 123 us
    pallas_call x1, Pallas kernels: 111 us -> 120 us  [owner_call(): pl.pallas_call(functools.partial(owner_kernel, n, rows, cols, cols // 4,...]
where the time goes in v7:
time: 126 us
  Pallas kernels  123 us (98%)
  local copies, waits for them, and re-layouts  2.24 us (2%)
    pallas_call x1, Pallas kernels, owner_call(): pl.pallas_call(functools.partial(owner_kernel, n, rows, cols, cols // 4,...  120 us
    pallas_call x1, Pallas kernels, master_call(): pl.pallas_call(functools.partial(master_kernel, n), out_shape=(jax.ShapeD...  3.34 us

profile of v7, /device:TPU:0, one launch (start us, length us, event | category | flops | bytes accessed | tf_op | source)
XLA Modules:
  0.0 125.9 jit_solution(4356621482872163290)
XLA Ops:
  0.6 0.0 copy-start.1
  0.6 0.6 copy-done.1
  1.3 0.0 copy-start.2
  1.3 1.6 %copy-done.2 = bf16[8,64,2048]{2,1,0:T(8,128)(2,1)S(1)} copy-done((bf16[8,64,2048]{2,1,0:T(8,128)(2,1)S(1)}, bf16[8,64,2048]{2,1,0:T(8,128)(2,1)}, u32[]{:S(2)}) %copy-start.2) | copy-done | bytes 2097176
  2.9 0.0 copy-start
  2.9 119.6 %shard_map.50 = (bf16[8,64,2048]{2,1,0:T(8,128)(2,1)S(1)}, bf16[512,2048]{1,0:T(8,128)(2,1)S(1)}) custom-call(s32[8]{0:T(128)S(1)} %copy-done.1, bf16[8,64,2048]{2,1,0:T(8,128)(2,1)S(1)} %copy-done.2), custom_call_target="tpu_custom_call" | custom-call | flops 8589934592 | bytes 12582912 | tf_op jit(solution)/shard_map/pallas_call | solution.py:273
  122.5 0.0 copy-done
  122.5 3.3 %shard_map.51 = (f32[8,64,2048]{2,1,0:T(8,128)}, bf16[512,2048]{1,0:T(8,128)(2,1)}) custom-call(s32[8]{0:T(128)S(1)} %copy-done.1, bf16[8,64,2048]{2,1,0:T(8,128)(2,1)S(1)} %get-tuple-element.6.ret_ref, bf16[512,2048]{1,0:T(8,128)(2,1)S(1)} %get-tuple-element.7.upd_ref, f32[8,64,2048]{2,1,0:T(8,128)S(1)} %copy-done), custom_call_target="tpu_custom_call" | custom-call | tf_op jit(solution)/shard_map/pallas_call | solution.py:322
Async XLA Ops:
  0.6 0.7 copy-start.1
  1.3 1.6 %copy-start.2 = (bf16[8,64,2048]{2,1,0:T(8,128)(2,1)S(1)}, bf16[8,64,2048]{2,1,0:T(8,128)(2,1)}, u32[]{:S(2)}) copy-start(bf16[8,64,2048]{2,1,0:T(8,128)(2,1)} %mom_ref.1) | copy-start | bytes 6291460
  2.9 119.6 %copy-start = (f32[8,64,2048]{2,1,0:T(8,128)S(1)}, f32[8,64,2048]{2,1,0:T(8,128)}, u32[]{:S(2)}) copy-start(f32[8,64,2048]{2,1,0:T(8,128)} %master_ref.1) | copy-start | bytes 12582916

commit v8 on v7

--- a/solution.py
+++ b/solution.py
@@ -35,8 +35,10 @@
 
 
 def visit_shifts(n):
-    shifts = [(pair, bit) for pair in range(1, n // 2) for bit in (0, 1)]
-    return shifts[:2] + [(0, 1)] + shifts[2:]
+    middle = n // 4
+    others = [pair for pair in range(1, n // 2) if pair != middle]
+    shifts = [(0, 1), (middle, 0), (middle, 1)]
+    return shifts + [(pair, bit) for bit in (0, 1) for pair in others]
 
 
 def owner_kernel(
@@ -74,12 +76,12 @@
         return 2 * lax.rem(pair + pairs - shift[0], pairs) + lax.rem(bit + shift[1], 2)
 
     def start_in_turn(slot, start):
-        if slot == 3:
-            pl.when(even)(lambda: start(3))
+        if slot == 1:
+            pl.when(even)(lambda: start(1))
         else:
             start(slot)
-        if slot == 5:
-            pl.when(jnp.logical_not(even))(lambda: start(3))
+        if slot == 2:
+            pl.when(jnp.logical_not(even))(lambda: start(1))
 
     barrier = pltpu.get_barrier_semaphore()
     for offset in range(1, n):

time: 126 us -> 117 us (0.929)
  the two profiles are of different devices: /device:TPU:0 before, /device:TPU:21 now
where the time goes in v8:
time: 117 us
  Pallas kernels  114 us (97%)
  local copies, waits for them, and re-layouts  2.24 us (2%)
    pallas_call x1, Pallas kernels, owner_call(): pl.pallas_call(functools.partial(owner_kernel, n, rows, cols, cols // 4,...  110 us
    pallas_call x1, Pallas kernels, master_call(): pl.pallas_call(functools.partial(master_kernel, n), out_shape=(jax.ShapeD...  3.34 us

profile of v8, /device:TPU:21, one launch (start us, length us, event | category | flops | bytes accessed | tf_op | source)
XLA Modules:
  0.0 116.5 jit_solution(3281388115819839234)
XLA Ops:
  0.6 0.0 copy-start.1
  0.6 0.6 copy-done.1
  1.3 0.0 copy-start.2
  1.3 1.6 %copy-done.2 = bf16[8,64,2048]{2,1,0:T(8,128)(2,1)S(1)} copy-done((bf16[8,64,2048]{2,1,0:T(8,128)(2,1)S(1)}, bf16[8,64,2048]{2,1,0:T(8,128)(2,1)}, u32[]{:S(2)}) %copy-start.2) | copy-done | bytes 2097176
  2.9 0.0 copy-start
  2.9 110.3 %shard_map.50 = (bf16[8,64,2048]{2,1,0:T(8,128)(2,1)S(1)}, bf16[512,2048]{1,0:T(8,128)(2,1)S(1)}) custom-call(s32[8]{0:T(128)S(1)} %copy-done.1, bf16[8,64,2048]{2,1,0:T(8,128)(2,1)S(1)} %copy-done.2), custom_call_target="tpu_custom_call" | custom-call | flops 8589934592 | bytes 12582912 | tf_op jit(solution)/shard_map/pallas_call | solution.py:275
  113.2 0.0 copy-done
  113.2 3.3 %shard_map.51 = (f32[8,64,2048]{2,1,0:T(8,128)}, bf16[512,2048]{1,0:T(8,128)(2,1)}) custom-call(s32[8]{0:T(128)S(1)} %copy-done.1, bf16[8,64,2048]{2,1,0:T(8,128)(2,1)S(1)} %get-tuple-element.6.ret_ref, bf16[512,2048]{1,0:T(8,128)(2,1)S(1)} %get-tuple-element.7.upd_ref, f32[8,64,2048]{2,1,0:T(8,128)S(1)} %copy-done), custom_call_target="tpu_custom_call" | custom-call | tf_op jit(solution)/shard_map/pallas_call | solution.py:324
Async XLA Ops:
  0.6 0.7 copy-start.1
  1.3 1.6 %copy-start.2 = (bf16[8,64,2048]{2,1,0:T(8,128)(2,1)S(1)}, bf16[8,64,2048]{2,1,0:T(8,128)(2,1)}, u32[]{:S(2)}) copy-start(bf16[8,64,2048]{2,1,0:T(8,128)(2,1)} %mom_ref.1) | copy-start | bytes 6291460
  2.9 110.3 %copy-start = (f32[8,64,2048]{2,1,0:T(8,128)S(1)}, f32[8,64,2048]{2,1,0:T(8,128)}, u32[]{:S(2)}) copy-start(f32[8,64,2048]{2,1,0:T(8,128)} %master_ref.1) | copy-start | bytes 12582916
